TPU v7x, 32 devices: a whole 2x2x4 slice. The times are simulated.
32 devices in a mesh: dp: 2 (over y), ctx: 4 (over z), tp: 4 (over x, core).
Axes of the slice: x: 2, y: 2, z: 4, core: 2. Of those that a mesh axis runs over, the one named last changes fastest.
Arguments:
- tokens: bfloat16 [1024, 4096], P(('dp', 'ctx'), 'tp'), parts along dimension 0, may hold values from -6 to 6
- expert_ids: int32 [1024, 8], P(('dp', 'ctx')), parts along dimension 0, may hold values from 0 to 127, all different within a row; in each aligned block of 128 rows (0 to 127, 128 to 255, ...) at most 16 rows name the same one
- route_weight: float32 [1024, 8], P(('dp', 'ctx')), parts along dimension 0, may hold values from 0.1 to 1
- gate_weight: bfloat16 [16, 384, 4096], P(('ctx', 'tp')), may hold values from -0.09375 to 0.09375
- up_weight: bfloat16 [16, 384, 4096], P(('ctx', 'tp')), may hold values from -0.09375 to 0.09375
- down_weight: bfloat16 [16, 384, 4096], P(('ctx', 'tp')), may hold values from -0.15625 to 0.15625
Outputs:
- mixed_out: bfloat16 [1024, 4096], P(('dp', 'ctx'), 'tp'), parts along dimension 0
There are 2 independent parts, one for each index of `dp`. A program takes and returns all parts, laid end to end along the dimension named above; an argument that names none is the same for every part. Nothing has to cross between parts.
Inputs may be any that keep to these rules, and one draw needn't show every extreme that they name: `expert_ids`: each token names 8 different experts. In each aligned block of 128 tokens no expert is named by more than 16 tokens, a bound that some block reaches.
All inputs are finite; a program needn't handle non-finite values.
Results may differ from a plain program's by a relative error of at most 0.018.
Values may be sent and summed in bfloat16 or wider, within the bound.
No kernel may reach another device: no remote copies, remote signals or barrier semaphores. Data moves between devices by JAX's collectives and lax.ppermute only.
A program may use at most 128 MiB of HBM per device.

v0:
```python
import jax
import jax.numpy as jnp
from jax import lax
from jax.sharding import PartitionSpec as P

SPLIT = 4
CAP = 16


def shards(tokens, expert_ids, route_weight, gate_weight, up_weight, down_weight):
    tok_rows = tokens.shape[0]
    route_count = expert_ids.shape[1]
    ctx_size = lax.axis_size("ctx")
    tp_size = lax.axis_size("tp")
    groups = tp_size // SPLIT
    exp_window = ctx_size * groups
    capacity = CAP
    whole = lax.all_gather(tokens, "tp", axis=1, tiled=True)
    full_width = whole.shape[1]
    flat_ids = expert_ids.reshape(-1)
    live_route = flat_ids < exp_window
    expert_marks = (flat_ids[:, None] == jnp.arange(exp_window, dtype=jnp.int32)[None, :]).astype(
        jnp.int32
    )
    running = jnp.cumsum(expert_marks, axis=0, dtype=jnp.int32) - 1
    slot_index = jnp.sum(running * expert_marks, axis=1, dtype=jnp.int32)
    target_row = jnp.where(live_route, flat_ids * capacity + slot_index, -1)
    place_index = jnp.arange(exp_window * capacity, dtype=jnp.int32)
    select_mask = (target_row[None, :] == place_index[:, None]).astype(jnp.float32)
    select_mask = select_mask.reshape(exp_window * capacity, tok_rows, route_count)
    pick_all = jnp.sum(select_mask, axis=2).reshape(ctx_size, groups, capacity, tok_rows)
    weight_all = jnp.sum(select_mask * route_weight.reshape(1, tok_rows, route_count), axis=2)
    weight_all = weight_all.reshape(ctx_size, groups, capacity, tok_rows)
    my_group = lax.axis_index("tp") // SPLIT
    pick_mine = (
        jnp.take(pick_all, my_group, axis=1)
        .reshape(ctx_size * capacity, tok_rows)
        .astype(jnp.bfloat16)
    )
    outgoing = jnp.dot(pick_mine, whole, preferred_element_type=jnp.float32).astype(jnp.bfloat16)
    outgoing = outgoing.reshape(ctx_size, capacity, full_width)
    arrived = lax.all_to_all(outgoing, "ctx", split_axis=0, concat_axis=0, tiled=True)
    gate_vals = jnp.einsum(
        "scd,fd->scf", arrived, gate_weight[0], preferred_element_type=jnp.float32
    )
    up_vals = jnp.einsum("scd,fd->scf", arrived, up_weight[0], preferred_element_type=jnp.float32)
    hidden = (jax.nn.silu(gate_vals) * up_vals).astype(jnp.bfloat16)
    part_out = jnp.einsum("scf,fd->scd", hidden, down_weight[0], preferred_element_type=jnp.float32)
    part_out = part_out.astype(jnp.bfloat16)
    back = lax.all_to_all(part_out, "ctx", split_axis=0, concat_axis=0, tiled=True)
    weight_mine = jnp.take(weight_all, my_group, axis=1).reshape(ctx_size * capacity, tok_rows)
    term = jnp.dot(
        weight_mine.T,
        back.reshape(-1, full_width).astype(jnp.float32),
        precision=lax.Precision.HIGHEST,
    )
    mixed_out = lax.psum_scatter(term.astype(jnp.bfloat16), "tp", scatter_dimension=1, tiled=True)
    return mixed_out


def solution(mesh):
    return jax.shard_map(
        shards,
        mesh=mesh,
        in_specs=(
            P(("dp", "ctx"), "tp"),
            P(("dp", "ctx"), None),
            P(("dp", "ctx"), None),
            P(("ctx", "tp"), None, None),
            P(("ctx", "tp"), None, None),
            P(("ctx", "tp"), None, None),
        ),
        out_specs=P(("dp", "ctx"), "tp"),
        check_vma=False,
    )
```

profile of v0, /device:TPU:0, one launch (start us, length us, event | category | flops | bytes accessed | tf_op | source)
XLA Modules:
  0.0 109.4 jit_solution(9555157457634530401)
XLA Ops:
  6.5 0.0 copy-start
  6.5 0.0 all-gather.2.cloned.1.call-start
  6.5 0.7 all-gather.2.cloned.1.call-update
  7.3 1.0 copy.23
  8.3 0.1 eq.43
  8.4 0.1 eq.39
  8.5 1.1 %reduce-window.6 = s32[4,8,128]{2,1,0:T(8,128)S(1)} reduce-window(s32[4,8,128]{2,1,0:T(8,128)S(1)} %fusion.23, s32[]{:T(128)} %constant.45.clone.1), window={size=1x1x128 pad=0_0x0_0x127_0}, to_apply=%region_0.0 | reduce-window | flops 520192 | bytes 32772 | tf_op jit(solution)/shard_map/reduce-window
  9.6 0.2 slice_reduce_fusion
  9.8 0.2 reduce-window.9
  10.0 0.1 add_bitcast_fusion
  10.1 0.1 reduce_sum.30
  10.3 0.7 add_select_fusion
  11.0 0.8 convert_reduce_fusion
  11.8 16.6 %all-gather.2.cloned.1.call-done = bf16[128,4096]{1,0:T(8,128)(2,1)} async-done(((bf16[128,1024]{1,0:T(8,128)(2,1)}), bf16[128,4096]{1,0:T(8,128)(2,1)}) %all-gather.2.cloned.1.call-update) | async-done | bytes 1048592 | tf_op jit(solution)/shard_map/all_gather | solution.py:18
  28.4 1.5 %convolution_convert_fusion.1 = bf16[64,4096]{1,0:T(8,128)(2,1)S(1)} fusion(bf16[128,4096]{1,0:T(8,128)(2,1)} %all-gather.2.cloned.1.call-done, bf16[64,128]{1,0:T(8,128)(2,1)S(1)} %get-tuple-element.5, pred[]{:T(512)S(6)} %and.13), kind=kOutput, calls=%fused_computation.3 | convolution fusion | flops 67379200 | bytes 1589249 | tf_op jit(solution)/shard_map/dot_general | solution.py:40
  29.9 19.3 %all_to_all.10 = bf16[4,16,4096]{2,1,0:T(8,128)(2,1)S(1)} all-to-all(bf16[4,16,4096]{2,1,0:T(8,128)(2,1)S(1)} %bitcast.44), channel_id=1, replica_groups=mesh['dp'=2,'ctx'=4,'tp'=4] {'ctx'}, dimensions={0} | all-to-all | bytes 1048576 | tf_op jit(solution)/shard_map/all_to_all | solution.py:42
  49.2 0.0 copy-start.1
  49.2 0.8 copy-done.1
  50.0 3.0 %fusion.4 = f32[4,16,384]{2,1,0:T(8,128)S(1)} fusion(bf16[4,16,4096]{2,1,0:T(8,128)(2,1)S(1)} %all_to_all.10, bf16[1,384,4096]{2,1,0:T(8,128)(2,1)} %param.9), kind=kOutput, calls=%fused_computation.7 | convolution fusion | flops 201326592 | bytes 3768320 | tf_op jit(solution)/shard_map/scd,fd->scf/dot_general | solution.py:43
  53.0 0.0 copy-done
  53.0 5.0 %convolution_convert_fusion = bf16[4,16,4096]{2,1,0:T(8,128)(2,1)} fusion(bf16[1,384,4096]{2,1,0:T(8,128)(2,1)S(1)} %copy-done, bf16[4,16,4096]{2,1,0:T(8,128)(2,1)} %copy-done.1, bf16[1,384,4096]{2,1,0:T(8,128)(2,1)} %param.10, f32[4,16,384]{2,1,0:T(8,128)S(1)} %fusion.4), kind=kOutput, calls=%fused_computation.2 | convolution fusion | flops 403062784 | bytes 7438336 | tf_op jit(solution)/shard_map/scf,fd->scd/dot_general | solution.py:48
  58.0 4.1 %all-to-all-start.1 = ((bf16[4,16,4096]{2,1,0:T(8,128)(2,1)}), bf16[4,16,4096]{2,1,0:T(8,128)(2,1)}, u32[]{:S(2)}, u32[]{:S(2)}) async-start(bf16[4,16,4096]{2,1,0:T(8,128)(2,1)} %convolution_convert_fusion), calls=%async_computation.1 | async-start | bytes 1048576 | tf_op jit(solution)/shard_map/all_to_all | solution.py:50
  62.2 0.0 reduce-scatter.2.cloned.1.call-start
  62.2 14.0 %all-to-all-done.1 = bf16[4,16,4096]{2,1,0:T(8,128)(2,1)} async-done(((bf16[4,16,4096]{2,1,0:T(8,128)(2,1)}), bf16[4,16,4096]{2,1,0:T(8,128)(2,1)}, u32[]{:S(2)}, u32[]{:S(2)}) %all-to-all-start.1) | async-done | bytes 524320 | tf_op jit(solution)/shard_map/all_to_all | solution.py:50
  76.3 3.1 %fusion = bf16[128,4096]{1,0:T(8,128)(2,1)} fusion(f32[4,16,128]{2,1,0:T(8,128)S(1)} %bitcast.45, bf16[4,16,4096]{2,1,0:T(8,128)(2,1)} %all-to-all-done.1), kind=kOutput, calls=%fused_computation.1 | convolution fusion | flops 403177472 | bytes 1605632 | tf_op jit(solution)/shard_map/dot_general | solution.py:52
  79.3 0.0 reduce-scatter.2.cloned.1.call-update
  79.3 23.2 %reduce-scatter.2.cloned.1.call-done = bf16[128,1024]{1,0:T(8,128)(2,1)} async-done(((bf16[128,4096]{1,0:T(8,128)(2,1)}), bf16[128,1024]{1,0:T(8,128)(2,1)}) %reduce-scatter.2.cloned.1.call-update) | async-done | bytes 262160 | tf_op jit(solution)/shard_map/reduce_scatter | solution.py:57
  (4 shorter events, 0.1 us)
Async XLA Ops:
  6.5 46.5 %copy-start = (bf16[1,384,4096]{2,1,0:T(8,128)(2,1)S(1)}, bf16[1,384,4096]{2,1,0:T(8,128)(2,1)}, u32[]{:S(2)}) copy-start(bf16[1,384,4096]{2,1,0:T(8,128)(2,1)} %param.11) | copy-start | bytes 9437188
  6.5 21.9 %all-gather.2.cloned.1.call-start = ((), (), s32[]{:S(2)}) async-start(), calls=%async_computation.3 | async-start | bytes 1310720 | tf_op jit(solution)/shard_map/all_gather | solution.py:18
  49.2 0.8 copy-start.1
  58.0 18.2 %all-to-all-start.1 = ((bf16[4,16,4096]{2,1,0:T(8,128)(2,1)}), bf16[4,16,4096]{2,1,0:T(8,128)(2,1)}, u32[]{:S(2)}, u32[]{:S(2)}) async-start(bf16[4,16,4096]{2,1,0:T(8,128)(2,1)} %convolution_convert_fusion), calls=%async_computation.1 | async-start | bytes 1048576 | tf_op jit(solution)/shard_map/all_to_all | solution.py:50
  62.2 40.4 %reduce-scatter.2.cloned.1.call-start = ((), (), s32[]{:S(2)}) async-start(), calls=%async_computation.4 | async-start | bytes 1310720 | tf_op jit(solution)/shard_map/reduce_scatter | solution.py:57
Sparse Core Ops, SparseCore 0:
  8.9 19.4 all-gather.1
  79.5 23.0 reduce-scatter.1
where the time goes:
time: 110 us; the launch traced here: 109 us
  waiting for transfers between devices  54.6 us (50%)
  blocking collectives  19.3 us (18%)
  between operations  13.5 us (12%)
  matrix products  12.5 us (11%)
  starting transfers between devices  4.18 us (4%)
  other arithmetic  3 us (3%)
  local copies, waits for them, and re-layouts  2.33 us (2%)
    reduce_scatter x1, waiting for transfers between devices, shards(): lax.psum_scatter(term.astype(jnp.bfloat16), 'tp', scatter_dimension=1, ti...  23.2 us
    all_to_all x1, blocking collectives, shards(): lax.all_to_all(outgoing, 'ctx', split_axis=0, concat_axis=0, tiled=True)  19.3 us
    all_gather x1, waiting for transfers between devices, shards(): whole = lax.all_gather(tokens, 'tp', axis=1, tiled=True)  16.6 us
    all_to_all x1, waiting for transfers between devices, shards(): lax.all_to_all(part_out, 'ctx', split_axis=0, concat_axis=0, tiled=True)  14 us
    dot_general x1, matrix products, shards(): jnp.einsum('scf,fd->scd', hidden, down_weight[0], preferred_element_type=...  4.98 us
    all_to_all x1, starting transfers between devices, shards(): lax.all_to_all(part_out, 'ctx', split_axis=0, concat_axis=0, tiled=True)  4.13 us
    dot_general x1, matrix products, shards(): jnp.dot(weight_mine.T, back.reshape(-1, full_width).astype(jnp.float32),...  3.06 us
    dot_general x1, matrix products, shards(): jnp.einsum('scd,fd->scf', arrived, gate_weight[0], preferred_element_type...  2.97 us
  transfers between devices with their start and end apart: 3, of which 3 were waited for; matrix products, arithmetic and copies ran while one was open for 4% of the time, Pallas kernels for 0%

commit v1 on v0

v1 whole, which is shorter than its diff:
```python
import functools

import jax
import jax.numpy as jnp
from jax import lax
from jax.experimental import pallas as pl
from jax.experimental.pallas import tpu as pltpu
from jax.sharding import PartitionSpec as P

SPLIT = 4
CAP = 16
CORES = 2
F32 = jnp.float32
BF16 = jnp.bfloat16
VMEM = pl.BlockSpec(memory_space=pltpu.VMEM)
HBM = pl.BlockSpec(memory_space=pltpu.HBM)
NT = (((1,), (1,)), ((), ()))


def swaps(size, mask):
    return [(i, i ^ mask) for i in range(size)]


def turns(size):
    half = size // 2
    return [*range(size - 1, half, -1), *range(1, half), 0, half]


def sds(shape, dtype=BF16):
    return jax.ShapeDtypeStruct(shape, dtype)


def local(kernel, name, out_shape, args, unread=(), cost=0):
    specs = [pl.BlockSpec(memory_space=pl.ANY) if i in unread else VMEM for i in range(len(args))]
    moved = cost or sum(a.size * a.dtype.itemsize for a in args)
    return pl.pallas_call(
        kernel,
        out_shape=out_shape,
        in_specs=specs,
        out_specs=jax.tree.map(lambda _: VMEM, out_shape),
        compiler_params=pltpu.CompilerParams(vmem_limit_bytes=4 * 1024 * 1024),
        cost_estimate=pl.CostEstimate(flops=0, bytes_accessed=moved, transcendentals=0),
        name=name,
    )(*args)


def columns(mask, features):
    at = lax.axis_index("tp") ^ mask
    return pl.ds(pl.multiple_of(at * features, features), features)


def route_kernel(ctx_size, groups, ids_hbm, weight_hbm, tokens_hbm, combine_ref, *refs):
    *row_refs, ids_ref, weight_ref, tokens_ref, sems = refs
    copies = [
        pltpu.make_async_copy(source, target, sems.at[i])
        for i, (source, target) in enumerate(
            ((ids_hbm, ids_ref), (weight_hbm, weight_ref), (tokens_hbm, tokens_ref))
        )
    ]
    for copy in copies:
        copy.start()
    slots = groups * CAP
    top, tok_rows = ids_ref.shape
    places = ctx_size * slots
    here = lax.axis_index("ctx")
    place = lax.broadcasted_iota(jnp.int32, (places, tok_rows), 0)
    order = place // slots
    turn = jnp.zeros_like(place)
    for i, mask in enumerate(turns(ctx_size)):
        turn = jnp.where(order == i, mask, turn)
    expert = (turn ^ here) * groups + (place % slots) // CAP
    slot = (place % CAP).astype(F32)
    before = (
        lax.broadcasted_iota(jnp.int32, (tok_rows, tok_rows), 0)
        < lax.broadcasted_iota(jnp.int32, (tok_rows, tok_rows), 1)
    ).astype(BF16)
    member = jnp.zeros((places, tok_rows), F32)
    weight = jnp.zeros((places, tok_rows), F32)
    copies[0].wait()
    copies[1].wait()
    for k in range(top):
        hit = ids_ref[k : k + 1, :] == expert
        member = jnp.where(hit, 1.0, member)
        weight = jnp.where(hit, weight_ref[k : k + 1, :], weight)
    running = jnp.dot(member.astype(BF16), before, preferred_element_type=F32)
    picked = jnp.where(running == slot, member, 0.0)
    combine_ref[...] = picked * weight
    copies[2].wait()
    rows = jnp.dot(picked.astype(BF16), tokens_ref[...], preferred_element_type=F32).astype(BF16)
    for s, ref in enumerate(row_refs):
        ref[...] = rows[s * slots : (s + 1) * slots]


def route(ids_t, weight_t, tokens, ctx_size, groups):
    tok_rows, features = tokens.shape
    slots = groups * CAP
    args = (ids_t, weight_t, tokens)
    return pl.pallas_call(
        functools.partial(route_kernel, ctx_size, groups),
        out_shape=[sds((ctx_size * slots, tok_rows), F32)] + [sds((slots, features))] * ctx_size,
        in_specs=[HBM] * 3,
        out_specs=[VMEM] * (ctx_size + 1),
        scratch_shapes=[pltpu.VMEM(a.shape, a.dtype) for a in args]
        + [pltpu.SemaphoreType.DMA((3,))],
        compiler_params=pltpu.CompilerParams(vmem_limit_bytes=4 * 1024 * 1024),
        name="route",
    )(*[pltpu.with_memory_space_constraint(a, pltpu.HBM) for a in args])


def load_gate_kernel(cuts, gate_hbm, combine_ref, gate_ref, mix_ref, sems):
    step = gate_ref.shape[0] // cuts
    copies = []
    for c in range(cuts):
        part = pl.ds(c * step, step)
        copies.append(pltpu.make_async_copy(gate_hbm.at[0, part], gate_ref.at[part], sems.at[c]))
    for copy in copies:
        copy.start()
    weight = combine_ref[...].T
    high = weight.astype(BF16)
    mix_ref[...] = jnp.concatenate([high, (weight - high.astype(F32)).astype(BF16)], axis=1)
    for copy in copies:
        copy.wait()


def load_gate(gate_weight, weights, cuts=4):
    places, tok_rows = weights.shape
    return pl.pallas_call(
        functools.partial(load_gate_kernel, cuts),
        out_shape=[sds(gate_weight.shape[1:]), sds((tok_rows, 2 * places))],
        in_specs=[HBM, VMEM],
        out_specs=[VMEM] * 2,
        scratch_shapes=[pltpu.SemaphoreType.DMA((cuts,))],
        compiler_params=pltpu.CompilerParams(vmem_limit_bytes=8 * 1024 * 1024),
        cost_estimate=pl.CostEstimate(
            flops=0, bytes_accessed=4 * gate_weight.size, transcendentals=0
        ),
        name="load_gate",
    )(pltpu.with_memory_space_constraint(gate_weight, pltpu.HBM), weights)


def mark_kernel(_, out_ref):
    out_ref[...] = jnp.zeros(out_ref.shape, F32)


def load_up_kernel(x_ref, gate_ref, up_hbm, up_ref, gate_out, up_out, sems):
    features = x_ref.shape[1]
    copies = []
    for mask in range(up_ref.shape[1] // features):
        part = columns(mask, features)
        copies.append(
            pltpu.make_async_copy(up_hbm.at[0, :, part], up_ref.at[:, part], sems.at[mask])
        )
    for copy in copies:
        copy.start()
    x = x_ref[...]
    own = columns(0, features)
    gate_out[...] = lax.dot_general(gate_ref[:, own], x, NT, preferred_element_type=F32)
    copies[0].wait()
    up_out[...] = lax.dot_general(up_ref[:, own], x, NT, preferred_element_type=F32)
    for copy in copies[1:]:
        copy.wait()


def load_up(x, gate, up_weight):
    rows, features = x.shape
    units, width = gate.shape
    return pl.pallas_call(
        load_up_kernel,
        out_shape=[sds((units, width))] + [sds((units, rows), F32)] * 2,
        in_specs=[VMEM, VMEM, HBM],
        out_specs=[VMEM] * 3,
        scratch_shapes=[pltpu.SemaphoreType.DMA((width // features,))],
        compiler_params=pltpu.CompilerParams(vmem_limit_bytes=8 * 1024 * 1024),
        cost_estimate=pl.CostEstimate(
            flops=0, bytes_accessed=4 * up_weight.size, transcendentals=0
        ),
        name="load_up",
    )(x, gate, pltpu.with_memory_space_constraint(up_weight, pltpu.HBM))


def stack_kernel(places, *refs):
    out_ref = refs[-1]
    for place, ref in zip(places, refs[-1 - len(places) : -1]):
        out_ref[place * ref.shape[0] : (place + 1) * ref.shape[0], :] = ref[...]


def stack(pieces, name, after, places=None):
    places = places or list(range(len(pieces)))
    rows = len(pieces) * pieces[0].shape[0]
    return local(
        functools.partial(stack_kernel, places),
        name,
        sds((rows, pieces[0].shape[1])),
        (*after, *pieces),
        unread=range(len(after)),
    )


def grow(chunks, masks, gate_ref, up_ref, sums):
    gate_vals, up_vals = sums
    for ref, mask in zip(chunks, masks):
        own = columns(mask, ref.shape[1])
        x = ref[...]
        gate_part = lax.dot_general(gate_ref[:, own], x, NT, preferred_element_type=F32)
        up_part = lax.dot_general(up_ref[:, own], x, NT, preferred_element_type=F32)
        gate_vals = gate_vals + gate_part
        up_vals = up_vals + up_part
    return gate_vals, up_vals


def grow_kernel(masks, *refs):
    chunks, (gate_ref, up_ref, gate_in, up_in, gate_out, up_out) = refs[:-6], refs[-6:]
    sums = (gate_in[...], up_in[...])
    gate_out[...], up_out[...] = grow(chunks, masks, gate_ref, up_ref, sums)


def expert_kernel(masks, out_masks, *refs):
    chunks = refs[: len(masks)]
    gate_ref, up_ref, down_ref, gate_in, up_in, hidden_ref, out_ref = refs[len(masks) :]
    sums = (gate_in[...], up_in[...])
    gate_vals, up_vals = grow(chunks, masks, gate_ref, up_ref, sums)
    hidden = (gate_vals / (1.0 + jnp.exp(-gate_vals)) * up_vals).T.astype(BF16)
    hidden_ref[...] = hidden
    shrink(hidden, out_masks, down_ref, out_ref)


def shrink(hidden, masks, down_ref, out_ref):
    rows, features = hidden.shape[0], out_ref.shape[1]
    for i, mask in enumerate(masks):
        down = down_ref[:, columns(mask, features)]
        out = jnp.dot(hidden, down, preferred_element_type=F32)
        out_ref[i * rows : (i + 1) * rows, :] = out.astype(BF16)


def shrink_kernel(masks, hidden_ref, down_ref, *refs):
    out_ref = refs[-1]
    shrink(hidden_ref[...], masks, down_ref, out_ref)


def pair_kernel(rows, own_ref, other_ref, *out_refs):
    count = out_refs[0].shape[0]
    for j, ref in enumerate(out_refs):
        at = slice(j * rows, j * rows + count)
        ref[...] = (own_ref[at, :].astype(F32) + other_ref[at, :].astype(F32)).astype(BF16)


def tail_kernel(own_ref, other_ref, own_away_ref, other_away_ref, out_ref):
    rows = own_ref.shape[0]
    for j in range(out_ref.shape[0] // CAP):
        mine, others = (own_ref, other_ref) if j == 0 else (own_away_ref, other_away_ref)
        at = slice(max(j, 1) * rows - CAP, max(j, 1) * rows)
        total = mine[at, :].astype(F32) + others[at, :].astype(F32)
        out_ref[j * CAP : (j + 1) * CAP, :] = total.astype(BF16)


def split_kernel(in_ref, *out_refs):
    for j, ref in enumerate(out_refs):
        ref[...] = in_ref[j * CAP : (j + 1) * CAP, :]


def group_sums(groups, parts):
    chips = len(parts)
    chip = lax.axis_index("tp") // CORES
    per_group = chips // groups
    totals = []
    for g in range(groups):
        total = None
        for j, term in enumerate(parts):
            if groups > 1:
                term = jnp.where((chip ^ j) // per_group == g, term, 0.0)
            total = term if total is None else total + term
        totals.append(total.astype(BF16))
    return totals


def total_kernel(groups, chips, own_ref, other_ref, *refs):
    part_refs, out_refs = refs[: chips - 1], refs[chips - 1 :]
    count = part_refs[0].shape[0]
    parts = [own_ref[:count, :].astype(F32) + other_ref[:count, :].astype(F32)]
    parts += [ref[...].astype(F32) for ref in part_refs]
    for g, total in enumerate(group_sums(groups, parts)):
        for s, ref in enumerate(out_refs):
            ref[g * CAP : (g + 1) * CAP, :] = total[s * CAP : (s + 1) * CAP]


def combine_kernel(order, groups, cuts, mix_ref, *refs):
    out_hbm, out_ref, sems = refs[-3:]
    count = len(order)
    back_refs, part_refs = refs[:count], refs[count:-3]
    back_refs = [back_refs[i] for i in order]
    mix = mix_ref[...]
    step = out_ref.shape[1] // cuts
    copies = []
    for c in range(cuts):
        part = slice(c * step, (c + 1) * step)
        parts = [ref[:, part].astype(F32) for ref in part_refs]
        back = [ref[:, part] for ref in back_refs] + group_sums(groups, parts)
        back = jnp.concatenate(back * 2, axis=0)
        out_ref[:, part] = jnp.dot(mix, back, preferred_element_type=F32).astype(BF16)
        copies.append(
            pltpu.make_async_copy(out_ref.at[:, part], out_hbm.at[:, part], sems.at[c])
        )
        copies[c].start()
    for copy in copies:
        copy.wait()


def combine(mix, order, groups, backs, parts, cuts=2):
    shape = sds((mix.shape[0], backs[0].shape[1]))
    args = (mix, *backs, *parts)
    return pl.pallas_call(
        functools.partial(combine_kernel, order, groups, cuts),
        out_shape=shape,
        in_specs=[VMEM] * len(args),
        out_specs=HBM,
        scratch_shapes=[pltpu.VMEM(shape.shape, BF16), pltpu.SemaphoreType.DMA((cuts,))],
        compiler_params=pltpu.CompilerParams(vmem_limit_bytes=4 * 1024 * 1024),
        name="combine",
    )(*args)


def shards(tokens, expert_ids, route_weight, gate_weight, up_weight, down_weight):
    ctx_size = lax.axis_size("ctx")
    tp_size = lax.axis_size("tp")
    groups = tp_size // SPLIT
    chips = tp_size // CORES
    tok_rows, features = tokens.shape
    slots = groups * CAP
    rows = ctx_size * CAP
    units = gate_weight.shape[1]

    def over_ctx(array, mask):
        return lax.ppermute(array, "ctx", swaps(ctx_size, mask))

    def over_chips(array, mask):
        return lax.ppermute(array, "tp", swaps(tp_size, mask * CORES))

    def over_cores(array):
        return lax.ppermute(array, "tp", swaps(tp_size, 1))

    weights, *picked = route(expert_ids.T, route_weight.T, tokens, ctx_size, groups)
    masks = turns(ctx_size)
    half = ctx_size // 2
    gate, mix = load_gate(gate_weight, weights)
    blocks = [over_ctx(p, mask) if mask else p for p, mask in zip(picked, masks)]
    chip = lax.axis_index("tp") // CORES

    def stacked(mask, part, after):
        pieces = blocks[part]
        if groups > 1:
            group = (chip ^ mask) // (chips // groups)
            pieces = [lax.dynamic_slice_in_dim(p, group * CAP, CAP) for p in pieces]
        return stack(pieces, "stack_half", after)

    halves = (slice(half, ctx_size), slice(0, half))
    mine = [stacked(0, halves[0], ())]
    mark = local(
        mark_kernel, "mark", sds((8, 128), F32), (mine[0],), unread=(0,), cost=2**24
    )
    mine.append(stacked(0, halves[1], (mark, gate)))
    arriving = [
        [
            over_chips(mine[i] if groups == 1 else stacked(j, part, (mine[i],)), j)
            for i, part in enumerate(halves)
        ]
        for j in range(1, chips)
    ]
    near = [stack(mine, "stack_own", (), (1, 0))]
    far = [over_cores(near[0])]
    up, *part = load_up(near[0], gate, up_weight)
    down = pltpu.with_memory_space_constraint(down_weight[0], pltpu.VMEM)
    near += [stack(pair, "stack_near", (up, down), (1, 0)) for pair in arriving]
    far += [over_cores(chunk) for chunk in near[1:]]
    part = local(
        functools.partial(grow_kernel, [1] + [j * CORES for j in range(1, chips)]),
        "grow",
        [sds((units, rows), F32)] * 2,
        (far[0], *near[1:], gate, up, *part),
    )
    away = [j * CORES for j in range(1, chips)]
    hidden, given = local(
        functools.partial(expert_kernel, [m + 1 for m in away], [m + 1 for m in away]),
        "expert",
        [sds((rows, units)), sds((len(away) * rows, features))],
        (*far[1:], gate, up, down, *part),
    )

    def shrunk(masks, name, after=()):
        return local(
            functools.partial(shrink_kernel, masks),
            name,
            sds((len(masks) * rows, features)),
            (hidden, down, *after),
            unread=range(2, 2 + len(after)),
        )

    other_away = over_cores(given)
    own_away = shrunk(away, "own_away")
    leaving = local(
        functools.partial(pair_kernel, rows),
        "pair",
        [sds((rows - CAP, features))] * (chips - 1),
        (own_away, other_away),
    )
    parts = [over_chips(leaving[j - 1], j) for j in range(1, chips)]
    given = shrunk([1], "given", (own_away,))
    own = shrunk([0], "own", (given,))
    other = over_cores(stack((given,), "stack_given", (own, other_away)))
    tail = local(
        tail_kernel, "tail", sds((chips * CAP, features)), (own, other, own_away, other_away)
    )
    got = over_ctx(tail, masks[-1])
    sums = local(
        functools.partial(total_kernel, groups, chips),
        "total",
        [sds((slots, features))] * (ctx_size - 1),
        (own, other, *parts),
    )
    far_first = sorted(zip(masks, sums), key=lambda pair: -pair[0])
    backs = [over_ctx(p, turn) if turn else p for turn, p in far_first]
    place = {turn: i for i, (turn, _) in enumerate(far_first)}
    order = [place[turn] for turn in masks[:-1]]
    pieces = local(split_kernel, "split", [sds((CAP, features))] * chips, (got,))
    late = [pieces[0]] + [over_chips(pieces[j], j) for j in range(1, chips)]
    return combine(mix, order, groups, backs, late)


def solution(mesh):
    return jax.shard_map(
        shards,
        mesh=mesh,
        in_specs=(
            P(("dp", "ctx"), "tp"),
            P(("dp", "ctx"), None),
            P(("dp", "ctx"), None),
            P(("ctx", "tp"), None, None),
            P(("ctx", "tp"), None, None),
            P(("ctx", "tp"), None, None),
        ),
        out_specs=P(("dp", "ctx"), "tp"),
        check_vma=False,
    )
```

time: 110 us -> 32.3 us (0.29)
  waiting for transfers between devices: 54.6 us -> 6.49 us
  blocking collectives: 19.3 us -> 0 us
  between operations: 13.5 us -> 0.16 us
  matrix products: 12.5 us -> 0 us
  starting transfers between devices: 4.18 us -> 16.6 us
  Pallas kernels: 0 us -> 8.76 us
  other arithmetic: 3 us -> 0 us
  local copies, waits for them, and re-layouts: 2.33 us -> 0.09 us
    reduce_scatter x1 -> x0, waiting for transfers between devices: 23.2 us -> none  [shards(): lax.psum_scatter(term.astype(jnp.bfloat16), 'tp', scatter_dimension=1, ti...]
    all_to_all x1 -> x0, blocking collectives: 19.3 us -> none  [shards(): lax.all_to_all(outgoing, 'ctx', split_axis=0, concat_axis=0, tiled=True)]
    ppermute x0 -> x14, starting transfers between devices: none -> 16.6 us  [the longest x6 10.2 us: over_ctx(): return lax.ppermute(array, 'ctx', swaps(ctx_size, mask))]
    all_gather x1 -> x0, waiting for transfers between devices: 16.6 us -> none  [shards(): whole = lax.all_gather(tokens, 'tp', axis=1, tiled=True)]
    all_to_all x1 -> x0, waiting for transfers between devices: 14 us -> none  [shards(): lax.all_to_all(part_out, 'ctx', split_axis=0, concat_axis=0, tiled=True)]
    dot_general x4 -> x0, matrix products: 12.5 us -> none  [the longest x1 4.98 us: shards(): jnp.einsum('scf,fd->scd', hidden, down_weight[0], preferred_element_type=...]
    pallas_call x0 -> x19, Pallas kernels: none -> 8.76 us  [the longest x15 2.68 us: local(): pl.pallas_call(kernel, out_shape=out_shape, in_specs=specs, out_specs=jax...]
    ppermute x0 -> x14, waiting for transfers between devices: none -> 6.49 us  [the longest x4 2.89 us: over_chips(): return lax.ppermute(array, 'tp', swaps(tp_size, mask * CORES))]
  transfers between devices with their start and end apart: 3 -> 14, of which waited for: 3 -> 9; matrix products, arithmetic and copies ran while one was open for 4% -> 0% of each run, Pallas kernels for 0% -> 18%
where the time goes in v1:
time: 32.3 us; the launch traced here: 32.1 us
  starting transfers between devices  16.6 us (51%)
  Pallas kernels  8.76 us (27%)
  waiting for transfers between devices  6.49 us (20%)
    ppermute x6, starting transfers between devices, over_ctx(): return lax.ppermute(array, 'ctx', swaps(ctx_size, mask))  10.2 us
    ppermute x4, starting transfers between devices, over_chips(): return lax.ppermute(array, 'tp', swaps(tp_size, mask * CORES))  5.87 us
    ppermute x4, waiting for transfers between devices, over_chips(): return lax.ppermute(array, 'tp', swaps(tp_size, mask * CORES))  2.89 us
    ppermute x6, waiting for transfers between devices, over_ctx(): return lax.ppermute(array, 'ctx', swaps(ctx_size, mask))  2.84 us
    pallas_call x15, Pallas kernels, local(): pl.pallas_call(kernel, out_shape=out_shape, in_specs=specs, out_specs=jax...  2.68 us
    pallas_call x1, Pallas kernels, load_up(): pl.pallas_call(load_up_kernel, out_shape=[sds((units, width))] + [sds((un...  2.11 us
    pallas_call x1, Pallas kernels, load_gate(): pl.pallas_call(functools.partial(load_gate_kernel, cuts), out_shape=[sds(...  1.88 us
    pallas_call x1, Pallas kernels, route(): pl.pallas_call(functools.partial(route_kernel, ctx_size, groups), out_sha...  1.2 us
  transfers between devices with their start and end apart: 14, of which 9 were waited for; matrix products, arithmetic and copies ran while one was open for 0% of the time, Pallas kernels for 18%

profile of v1, /device:TPU:0, one launch (start us, length us, event | category | flops | bytes accessed | tf_op | source)
XLA Modules:
  0.0 32.1 jit_solution(2931472342934714701)
XLA Ops:
  0.0 1.2 %route.1 = (f32[64,128]{1,0:T(8,128)S(1)}, bf16[16,1024]{1,0:T(8,128)(2,1)S(1)}, bf16[16,1024]{1,0:T(8,128)(2,1)S(1)}, bf16[16,1024]{1,0:T(8,128)(2,1)S(1)}, bf16[16,1024]{1,0:T(8,128)(2,1)S(1)}) custom-call(s32[8,128]{1,0:T(8,128)} %bitcast.8, f32[8,128]{1,0:T(8,128)} %bitcast.9, bf16[128,1024]{1,0:T(8,128)(2,1)} %tokens_hbm.1), custom_call_target="tpu_custom_call" | custom-call | tf_op jit(solution)/shard_map/route/pallas_call | solution.py:98
  1.2 4.1 %collective-permute-start = (bf16[16,1024]{1,0:T(8,128)(2,1)S(1)}, bf16[16,1024]{1,0:T(8,128)(2,1)S(1)}, u32[]{:S(2)}, u32[]{:S(2)}) collective-permute-start(bf16[16,1024]{1,0:T(8,128)(2,1)S(1)} %get-tuple-element.27), channel_id=1, source_target_pairs={{0,8},{4,12},{8,0},{12,4},{1,9},{5,13},{9,1},{13,5},{2,10},{6,14},... | collective-permute-start | bytes 98312 | tf_op jit(solution)/shard_map/ppermute | solution.py:333
  5.3 1.3 %collective-permute-start.1 = (bf16[16,1024]{1,0:T(8,128)(2,1)S(1)}, bf16[16,1024]{1,0:T(8,128)(2,1)S(1)}, u32[]{:S(2)}, u32[]{:S(2)}) collective-permute-start(bf16[16,1024]{1,0:T(8,128)(2,1)S(1)} %get-tuple-element.29), channel_id=1, source_target_pairs={{0,12},{4,8},{8,4},{12,0},{1,13},{5,9},{9,5},{13,1},{2,14},{6,10},... | collective-permute-start | bytes 98312 | tf_op jit(solution)/shard_map/ppermute | solution.py:333
  6.7 0.2 collective-permute-start.2
  6.9 1.9 %load_gate.1 = (bf16[384,4096]{1,0:T(8,128)(2,1)S(1)}, bf16[128,128]{1,0:T(8,128)(2,1)S(1)}) custom-call(bf16[1,384,4096]{2,1,0:T(8,128)(2,1)} %gate_hbm.1, f32[64,128]{1,0:T(8,128)S(1)} %get-tuple-element.24.combine_ref), custom_call_target="tpu_custom_call" | custom-call | bytes 6291456 | tf_op jit(solution)/shard_map/load_gate/pallas_call | solution.py:127
  8.8 0.0 collective-permute-done.refs_1_
  8.8 1.6 %collective-permute-start.3 = (bf16[32,1024]{1,0:T(8,128)(2,1)S(1)}, bf16[32,1024]{1,0:T(8,128)(2,1)S(1)}, u32[]{:S(2)}, u32[]{:S(2)}) collective-permute-start(bf16[32,1024]{1,0:T(8,128)(2,1)S(1)} %stack_half.2._.refs_0_), channel_id=1, source_target_pairs={{0,2},{1,3},{2,0},{3,1},{4,6},{5,7},{6,4},{7,5},{8,10},{9,11},{10,... | collective-permute-start | bytes 196616 | tf_op jit(solution)/shard_map/ppermute | solution.py:336
  10.4 0.7 %collective-permute-done.1.refs_2_ = bf16[16,1024]{1,0:T(8,128)(2,1)S(1)} collective-permute-done((bf16[16,1024]{1,0:T(8,128)(2,1)S(1)}, bf16[16,1024]{1,0:T(8,128)(2,1)S(1)}, u32[]{:S(2)}, u32[]{:S(2)}) %collective-permute-start.1) | collective-permute-done | bytes 32800 | tf_op jit(solution)/shard_map/ppermute | solution.py:333
  11.0 0.0 collective-permute-done.2.refs_3_
  11.0 1.6 %collective-permute-start.4 = (bf16[32,1024]{1,0:T(8,128)(2,1)S(1)}, bf16[32,1024]{1,0:T(8,128)(2,1)S(1)}, u32[]{:S(2)}, u32[]{:S(2)}) collective-permute-start(bf16[32,1024]{1,0:T(8,128)(2,1)S(1)} %stack_half.3.refs_1_), channel_id=1, source_target_pairs={{0,2},{1,3},{2,0},{3,1},{4,6},{5,7},{6,4},{7,5},{8,10},{9,11},{10,... | collective-permute-start | bytes 196616 | tf_op jit(solution)/shard_map/ppermute | solution.py:336
  12.6 0.0 copy-start
  12.6 0.1 collective-permute-start.6
  12.7 2.1 %load_up.1 = (bf16[384,4096]{1,0:T(8,128)(2,1)S(1)}, f32[384,64]{1,0:T(8,128)S(1)}, f32[384,64]{1,0:T(8,128)S(1)}) custom-call(bf16[64,1024]{1,0:T(8,128)(2,1)S(1)} %stack_own.1.x_ref, bf16[384,4096]{1,0:T(8,128)(2,1)S(1)} %get-tuple-element.28.refs_1_.gate_ref.refs_2_, bf16[1,384,4096]{2,1,0:T(8,128)(2,1)} %up_hbm.1), custom_call_target="tpu_custom_call" | custom-call | bytes 6291456 | tf_op jit(solution)/shard_map/load_up/pallas_call | solution.py:167
  14.8 0.0 collective-permute-done.3.refs_2_
  14.8 0.5 %collective-permute-done.4.refs_3_ = bf16[32,1024]{1,0:T(8,128)(2,1)S(1)} collective-permute-done((bf16[32,1024]{1,0:T(8,128)(2,1)S(1)}, bf16[32,1024]{1,0:T(8,128)(2,1)S(1)}, u32[]{:S(2)}, u32[]{:S(2)}) %collective-permute-start.4) | collective-permute-done | bytes 65568 | tf_op jit(solution)/shard_map/ppermute | solution.py:336
  15.4 0.1 copy-done
  15.5 0.1 collective-permute-start.5
  15.5 0.0 collective-permute-done.6.refs_0_
  15.6 1.0 %grow.1 = (f32[384,64]{1,0:T(8,128)S(1)}, f32[384,64]{1,0:T(8,128)S(1)}) custom-call(bf16[64,1024]{1,0:T(8,128)(2,1)S(1)} %collective-permute-done.6.refs_0_, bf16[64,1024]{1,0:T(8,128)(2,1)S(1)} %stack_near.1.refs_1_, bf16[384,4096]{1,0:T(8,128)(2,1)S(1)} %get-tuple-element.28.refs_1_.gate_ref.refs_2_, ...), custom_call_target="tpu_custom_call" | custom-call | bytes 6750208 | tf_op jit(solution)/shard_map/grow/pallas_call | solution.py:36
  16.5 0.4 %collective-permute-done.5.refs_0_ = bf16[64,1024]{1,0:T(8,128)(2,1)S(1)} collective-permute-done((bf16[64,1024]{1,0:T(8,128)(2,1)S(1)}, bf16[64,1024]{1,0:T(8,128)(2,1)S(1)}, u32[]{:S(2)}, u32[]{:S(2)}) %collective-permute-start.5) | collective-permute-done | bytes 131104 | tf_op jit(solution)/shard_map/ppermute | solution.py:339
  16.9 0.8 %expert.1 = (bf16[64,384]{1,0:T(8,128)(2,1)S(1)}, bf16[64,1024]{1,0:T(8,128)(2,1)S(1)}) custom-call(bf16[64,1024]{1,0:T(8,128)(2,1)S(1)} %collective-permute-done.5.refs_0_, bf16[384,4096]{1,0:T(8,128)(2,1)S(1)} %get-tuple-element.28.refs_1_.gate_ref.refs_2_, bf16[384,4096]{1,0:T(8,128)(2,1)S(1)} %get-tuple-element.31.refs_0_.refs_3_.refs_2_, ...), custom_call_target="tpu_custom_call" | custom-call | bytes 9764864 | tf_op jit(solution)/shard_map/expert/pallas_call | solution.py:36
  17.7 0.2 collective-permute-start.7
  17.9 0.3 own_away.1.refs_0_.own_ref.own_away_ref
  18.2 0.3 given.1.refs_0_.refs_2_
  18.4 0.3 own.1.refs_0_.own_ref
  18.7 0.4 %collective-permute-done.7.refs_1_.other_ref.other_away_ref = bf16[64,1024]{1,0:T(8,128)(2,1)S(1)} collective-permute-done((bf16[64,1024]{1,0:T(8,128)(2,1)S(1)}, bf16[64,1024]{1,0:T(8,128)(2,1)S(1)}, u32[]{:S(2)}, u32[]{:S(2)}) %collective-permute-start.7) | collective-permute-done | bytes 131104 | tf_op jit(solution)/shard_map/ppermute | solution.py:339
  19.1 0.2 collective-permute-start.8
  19.4 1.5 %collective-permute-start.9 = (bf16[48,1024]{1,0:T(8,128)(2,1)S(1)}, bf16[48,1024]{1,0:T(8,128)(2,1)S(1)}, u32[]{:S(2)}, u32[]{:S(2)}) collective-permute-start(bf16[48,1024]{1,0:T(8,128)(2,1)S(1)} %pair.1), channel_id=1, source_target_pairs={{0,2},{1,3},{2,0},{3,1},{4,6},{5,7},{6,4},{7,5},{8,10},{9,11},{10,... | collective-permute-start | bytes 294920 | tf_op jit(solution)/shard_map/ppermute | solution.py:336
  20.8 0.0 collective-permute-done.8.other_ref
  20.9 1.8 %collective-permute-start.12 = (bf16[32,1024]{1,0:T(8,128)(2,1)S(1)}, bf16[32,1024]{1,0:T(8,128)(2,1)S(1)}, u32[]{:S(2)}, u32[]{:S(2)}) collective-permute-start(bf16[32,1024]{1,0:T(8,128)(2,1)S(1)} %tail.1), channel_id=1, source_target_pairs={{0,8},{4,12},{8,0},{12,4},{1,9},{5,13},{9,1},{13,5},{2,10},{6,14},... | collective-permute-start | bytes 196616 | tf_op jit(solution)/shard_map/ppermute | solution.py:333
  22.7 1.8 %collective-permute-done.9.refs_0_ = bf16[48,1024]{1,0:T(8,128)(2,1)S(1)} collective-permute-done((bf16[48,1024]{1,0:T(8,128)(2,1)S(1)}, bf16[48,1024]{1,0:T(8,128)(2,1)S(1)}, u32[]{:S(2)}, u32[]{:S(2)}) %collective-permute-start.9) | collective-permute-done | bytes 98336 | tf_op jit(solution)/shard_map/ppermute | solution.py:336
  24.5 2.2 %collective-permute-start.10 = (bf16[16,1024]{1,0:T(8,128)(2,1)S(1)}, bf16[16,1024]{1,0:T(8,128)(2,1)S(1)}, u32[]{:S(2)}, u32[]{:S(2)}) collective-permute-start(bf16[16,1024]{1,0:T(8,128)(2,1)S(1)} %get-tuple-element.38), channel_id=1, source_target_pairs={{0,12},{4,8},{8,4},{12,0},{1,13},{5,9},{9,5},{13,1},{2,14},{6,10},... | collective-permute-start | bytes 98312 | tf_op jit(solution)/shard_map/ppermute | solution.py:333
  26.8 0.4 %collective-permute-start.11 = (bf16[16,1024]{1,0:T(8,128)(2,1)S(1)}, bf16[16,1024]{1,0:T(8,128)(2,1)S(1)}, u32[]{:S(2)}, u32[]{:S(2)}) collective-permute-start(bf16[16,1024]{1,0:T(8,128)(2,1)S(1)} %get-tuple-element.39), channel_id=1, source_target_pairs={{0,4},{4,0},{8,12},{12,8},{1,5},{5,1},{9,13},{13,9},{2,6},{6,2},{1... | collective-permute-start | bytes 98312 | tf_op jit(solution)/shard_map/ppermute | solution.py:333
  27.2 0.1 collective-permute-done.12.in_ref
  27.3 1.3 %collective-permute-start.13 = (bf16[16,1024]{1,0:T(8,128)(2,1)S(1)}, bf16[16,1024]{1,0:T(8,128)(2,1)S(1)}, u32[]{:S(2)}, u32[]{:S(2)}) collective-permute-start(bf16[16,1024]{1,0:T(8,128)(2,1)S(1)} %get-tuple-element.42), channel_id=1, source_target_pairs={{0,2},{1,3},{2,0},{3,1},{4,6},{5,7},{6,4},{7,5},{8,10},{9,11},{10,... | collective-permute-start | bytes 98312 | tf_op jit(solution)/shard_map/ppermute | solution.py:336
  28.6 1.7 %collective-permute-done.10.refs_0_ = bf16[16,1024]{1,0:T(8,128)(2,1)S(1)} collective-permute-done((bf16[16,1024]{1,0:T(8,128)(2,1)S(1)}, bf16[16,1024]{1,0:T(8,128)(2,1)S(1)}, u32[]{:S(2)}, u32[]{:S(2)}) %collective-permute-start.10) | collective-permute-done | bytes 32800 | tf_op jit(solution)/shard_map/ppermute | solution.py:333
  30.3 0.4 %collective-permute-done.11.refs_1_ = bf16[16,1024]{1,0:T(8,128)(2,1)S(1)} collective-permute-done((bf16[16,1024]{1,0:T(8,128)(2,1)S(1)}, bf16[16,1024]{1,0:T(8,128)(2,1)S(1)}, u32[]{:S(2)}, u32[]{:S(2)}) %collective-permute-start.11) | collective-permute-done | bytes 32800 | tf_op jit(solution)/shard_map/ppermute | solution.py:333
  30.7 0.5 %collective-permute-done.13.refs_4_ = bf16[16,1024]{1,0:T(8,128)(2,1)S(1)} collective-permute-done((bf16[16,1024]{1,0:T(8,128)(2,1)S(1)}, bf16[16,1024]{1,0:T(8,128)(2,1)S(1)}, u32[]{:S(2)}, u32[]{:S(2)}) %collective-permute-start.13) | collective-permute-done | bytes 32800 | tf_op jit(solution)/shard_map/ppermute | solution.py:336
  31.2 0.9 %combine.1 = bf16[128,1024]{1,0:T(8,128)(2,1)} custom-call(bf16[128,128]{1,0:T(8,128)(2,1)S(1)} %get-tuple-element.25.mix_ref, bf16[16,1024]{1,0:T(8,128)(2,1)S(1)} %collective-permute-done.10.refs_0_, bf16[16,1024]{1,0:T(8,128)(2,1)S(1)} %collective-permute-done.11.refs_1_, bf16[16,1024]{1,0:T(8,128)(2,1)S(1)} %get-tuple-element.40.refs_2_, ...), custom_call_target="tpu_custom_call" | custom-call | tf_op jit(solution)/shard_map/combine/pallas_call | solution.py:311
  (10 shorter events, 0.1 us)
Async XLA Ops:
  1.2 7.6 %collective-permute-start = (bf16[16,1024]{1,0:T(8,128)(2,1)S(1)}, bf16[16,1024]{1,0:T(8,128)(2,1)S(1)}, u32[]{:S(2)}, u32[]{:S(2)}) collective-permute-start(bf16[16,1024]{1,0:T(8,128)(2,1)S(1)} %get-tuple-element.27), channel_id=1, source_target_pairs={{0,8},{4,12},{8,0},{12,4},{1,9},{5,13},{9,1},{13,5},{2,10},{6,14},... | collective-permute-start | bytes 98312 | tf_op jit(solution)/shard_map/ppermute | solution.py:333
  5.3 5.7 %collective-permute-start.1 = (bf16[16,1024]{1,0:T(8,128)(2,1)S(1)}, bf16[16,1024]{1,0:T(8,128)(2,1)S(1)}, u32[]{:S(2)}, u32[]{:S(2)}) collective-permute-start(bf16[16,1024]{1,0:T(8,128)(2,1)S(1)} %get-tuple-element.29), channel_id=1, source_target_pairs={{0,12},{4,8},{8,4},{12,0},{1,13},{5,9},{9,5},{13,1},{2,14},{6,10},... | collective-permute-start | bytes 98312 | tf_op jit(solution)/shard_map/ppermute | solution.py:333
  6.7 4.4 %collective-permute-start.2 = (bf16[16,1024]{1,0:T(8,128)(2,1)S(1)}, bf16[16,1024]{1,0:T(8,128)(2,1)S(1)}, u32[]{:S(2)}, u32[]{:S(2)}) collective-permute-start(bf16[16,1024]{1,0:T(8,128)(2,1)S(1)} %get-tuple-element.30), channel_id=1, source_target_pairs={{0,4},{4,0},{8,12},{12,8},{1,5},{5,1},{9,13},{13,9},{2,6},{6,2},{1... | collective-permute-start | bytes 98312 | tf_op jit(solution)/shard_map/ppermute | solution.py:333
  8.8 6.0 %collective-permute-start.3 = (bf16[32,1024]{1,0:T(8,128)(2,1)S(1)}, bf16[32,1024]{1,0:T(8,128)(2,1)S(1)}, u32[]{:S(2)}, u32[]{:S(2)}) collective-permute-start(bf16[32,1024]{1,0:T(8,128)(2,1)S(1)} %stack_half.2._.refs_0_), channel_id=1, source_target_pairs={{0,2},{1,3},{2,0},{3,1},{4,6},{5,7},{6,4},{7,5},{8,10},{9,11},{10,... | collective-permute-start | bytes 196616 | tf_op jit(solution)/shard_map/ppermute | solution.py:336
  11.0 4.3 %collective-permute-start.4 = (bf16[32,1024]{1,0:T(8,128)(2,1)S(1)}, bf16[32,1024]{1,0:T(8,128)(2,1)S(1)}, u32[]{:S(2)}, u32[]{:S(2)}) collective-permute-start(bf16[32,1024]{1,0:T(8,128)(2,1)S(1)} %stack_half.3.refs_1_), channel_id=1, source_target_pairs={{0,2},{1,3},{2,0},{3,1},{4,6},{5,7},{6,4},{7,5},{8,10},{9,11},{10,... | collective-permute-start | bytes 196616 | tf_op jit(solution)/shard_map/ppermute | solution.py:336
  12.6 2.9 %copy-start = (bf16[1,384,4096]{2,1,0:T(8,128)(2,1)S(1)}, bf16[1,384,4096]{2,1,0:T(8,128)(2,1)}, u32[]{:S(2)}) copy-start(bf16[1,384,4096]{2,1,0:T(8,128)(2,1)} %param.11) | copy-start | bytes 9437188
  12.6 2.9 %collective-permute-start.6 = (bf16[64,1024]{1,0:T(8,128)(2,1)S(1)}, bf16[64,1024]{1,0:T(8,128)(2,1)S(1)}, u32[]{:S(2)}, u32[]{:S(2)}) collective-permute-start(bf16[64,1024]{1,0:T(8,128)(2,1)S(1)} %stack_own.1.x_ref), channel_id=1, source_target_pairs={{0,1},{1,0},{2,3},{3,2},{4,5},{5,4},{6,7},{7,6},{8,9},{9,8},{10,11... | collective-permute-start | bytes 393224 | tf_op jit(solution)/shard_map/ppermute | solution.py:339
  15.5 1.4 %collective-permute-start.5 = (bf16[64,1024]{1,0:T(8,128)(2,1)S(1)}, bf16[64,1024]{1,0:T(8,128)(2,1)S(1)}, u32[]{:S(2)}, u32[]{:S(2)}) collective-permute-start(bf16[64,1024]{1,0:T(8,128)(2,1)S(1)} %stack_near.1.refs_1_), channel_id=1, source_target_pairs={{0,1},{1,0},{2,3},{3,2},{4,5},{5,4},{6,7},{7,6},{8,9},{9,8},{10,11... | collective-permute-start | bytes 393224 | tf_op jit(solution)/shard_map/ppermute | solution.py:339
  17.7 1.4 %collective-permute-start.7 = (bf16[64,1024]{1,0:T(8,128)(2,1)S(1)}, bf16[64,1024]{1,0:T(8,128)(2,1)S(1)}, u32[]{:S(2)}, u32[]{:S(2)}) collective-permute-start(bf16[64,1024]{1,0:T(8,128)(2,1)S(1)} %get-tuple-element.37), channel_id=1, source_target_pairs={{0,1},{1,0},{2,3},{3,2},{4,5},{5,4},{6,7},{7,6},{8,9},{9,8},{10,11... | collective-permute-start | bytes 393224 | tf_op jit(solution)/shard_map/ppermute | solution.py:339
  19.1 1.7 %collective-permute-start.8 = (bf16[64,1024]{1,0:T(8,128)(2,1)S(1)}, bf16[64,1024]{1,0:T(8,128)(2,1)S(1)}, u32[]{:S(2)}, u32[]{:S(2)}) collective-permute-start(bf16[64,1024]{1,0:T(8,128)(2,1)S(1)} %stack_given.1), channel_id=1, source_target_pairs={{0,1},{1,0},{2,3},{3,2},{4,5},{5,4},{6,7},{7,6},{8,9},{9,8},{10,11... | collective-permute-start | bytes 393224 | tf_op jit(solution)/shard_map/ppermute | solution.py:339
  19.4 5.1 %collective-permute-start.9 = (bf16[48,1024]{1,0:T(8,128)(2,1)S(1)}, bf16[48,1024]{1,0:T(8,128)(2,1)S(1)}, u32[]{:S(2)}, u32[]{:S(2)}) collective-permute-start(bf16[48,1024]{1,0:T(8,128)(2,1)S(1)} %pair.1), channel_id=1, source_target_pairs={{0,2},{1,3},{2,0},{3,1},{4,6},{5,7},{6,4},{7,5},{8,10},{9,11},{10,... | collective-permute-start | bytes 294920 | tf_op jit(solution)/shard_map/ppermute | solution.py:336
  20.9 6.4 %collective-permute-start.12 = (bf16[32,1024]{1,0:T(8,128)(2,1)S(1)}, bf16[32,1024]{1,0:T(8,128)(2,1)S(1)}, u32[]{:S(2)}, u32[]{:S(2)}) collective-permute-start(bf16[32,1024]{1,0:T(8,128)(2,1)S(1)} %tail.1), channel_id=1, source_target_pairs={{0,8},{4,12},{8,0},{12,4},{1,9},{5,13},{9,1},{13,5},{2,10},{6,14},... | collective-permute-start | bytes 196616 | tf_op jit(solution)/shard_map/ppermute | solution.py:333
  24.5 5.8 %collective-permute-start.10 = (bf16[16,1024]{1,0:T(8,128)(2,1)S(1)}, bf16[16,1024]{1,0:T(8,128)(2,1)S(1)}, u32[]{:S(2)}, u32[]{:S(2)}) collective-permute-start(bf16[16,1024]{1,0:T(8,128)(2,1)S(1)} %get-tuple-element.38), channel_id=1, source_target_pairs={{0,12},{4,8},{8,4},{12,0},{1,13},{5,9},{9,5},{13,1},{2,14},{6,10},... | collective-permute-start | bytes 98312 | tf_op jit(solution)/shard_map/ppermute | solution.py:333
  26.8 3.9 %collective-permute-start.11 = (bf16[16,1024]{1,0:T(8,128)(2,1)S(1)}, bf16[16,1024]{1,0:T(8,128)(2,1)S(1)}, u32[]{:S(2)}, u32[]{:S(2)}) collective-permute-start(bf16[16,1024]{1,0:T(8,128)(2,1)S(1)} %get-tuple-element.39), channel_id=1, source_target_pairs={{0,4},{4,0},{8,12},{12,8},{1,5},{5,1},{9,13},{13,9},{2,6},{6,2},{1... | collective-permute-start | bytes 98312 | tf_op jit(solution)/shard_map/ppermute | solution.py:333
  27.3 3.9 %collective-permute-start.13 = (bf16[16,1024]{1,0:T(8,128)(2,1)S(1)}, bf16[16,1024]{1,0:T(8,128)(2,1)S(1)}, u32[]{:S(2)}, u32[]{:S(2)}) collective-permute-start(bf16[16,1024]{1,0:T(8,128)(2,1)S(1)} %get-tuple-element.42), channel_id=1, source_target_pairs={{0,2},{1,3},{2,0},{3,1},{4,6},{5,7},{6,4},{7,5},{8,10},{9,11},{10,... | collective-permute-start | bytes 98312 | tf_op jit(solution)/shard_map/ppermute | solution.py:336

commit v2 on v1

--- a/solution.py
+++ b/solution.py
@@ -107,12 +107,12 @@
     )(*[pltpu.with_memory_space_constraint(a, pltpu.HBM) for a in args])
 
 
-def load_gate_kernel(cuts, gate_hbm, combine_ref, gate_ref, mix_ref, sems):
-    step = gate_ref.shape[0] // cuts
+def load_gate_kernel(cuts, gate_hbm, combine_ref, both_ref, mix_ref, sems):
+    step = gate_hbm.shape[1] // cuts
     copies = []
     for c in range(cuts):
         part = pl.ds(c * step, step)
-        copies.append(pltpu.make_async_copy(gate_hbm.at[0, part], gate_ref.at[part], sems.at[c]))
+        copies.append(pltpu.make_async_copy(gate_hbm.at[0, part], both_ref.at[part], sems.at[c]))
     for copy in copies:
         copy.start()
     weight = combine_ref[...].T
@@ -124,13 +124,14 @@
 
 def load_gate(gate_weight, weights, cuts=4):
     places, tok_rows = weights.shape
+    _, units, width = gate_weight.shape
     return pl.pallas_call(
         functools.partial(load_gate_kernel, cuts),
-        out_shape=[sds(gate_weight.shape[1:]), sds((tok_rows, 2 * places))],
+        out_shape=[sds((2 * units, width)), sds((tok_rows, 2 * places))],
         in_specs=[HBM, VMEM],
         out_specs=[VMEM] * 2,
         scratch_shapes=[pltpu.SemaphoreType.DMA((cuts,))],
-        compiler_params=pltpu.CompilerParams(vmem_limit_bytes=8 * 1024 * 1024),
+        compiler_params=pltpu.CompilerParams(vmem_limit_bytes=12 * 1024 * 1024),
         cost_estimate=pl.CostEstimate(
             flops=0, bytes_accessed=4 * gate_weight.size, transcendentals=0
         ),
@@ -142,40 +143,52 @@
     out_ref[...] = jnp.zeros(out_ref.shape, F32)
 
 
-def load_up_kernel(x_ref, gate_ref, up_hbm, up_ref, gate_out, up_out, sems):
+def load_up_kernel(x_ref, _, up_hbm, both_ref, sums_out, sems):
     features = x_ref.shape[1]
+    units = up_hbm.shape[1]
     copies = []
-    for mask in range(up_ref.shape[1] // features):
+    for mask in range(both_ref.shape[1] // features):
         part = columns(mask, features)
         copies.append(
-            pltpu.make_async_copy(up_hbm.at[0, :, part], up_ref.at[:, part], sems.at[mask])
+            pltpu.make_async_copy(
+                up_hbm.at[0, :, part], both_ref.at[units:, part], sems.at[mask]
+            )
         )
     for copy in copies:
         copy.start()
     x = x_ref[...]
     own = columns(0, features)
-    gate_out[...] = lax.dot_general(gate_ref[:, own], x, NT, preferred_element_type=F32)
+    sums_out[:units, :] = lax.dot_general(
+        both_ref[:units, own], x, NT, preferred_element_type=F32
+    )
     copies[0].wait()
-    up_out[...] = lax.dot_general(up_ref[:, own], x, NT, preferred_element_type=F32)
+    sums_out[units:, :] = lax.dot_general(
+        both_ref[units:, own], x, NT, preferred_element_type=F32
+    )
     for copy in copies[1:]:
         copy.wait()
 
 
-def load_up(x, gate, up_weight):
+def load_up(x, both, up_weight):
     rows, features = x.shape
-    units, width = gate.shape
+    units, width = both.shape
     return pl.pallas_call(
         load_up_kernel,
-        out_shape=[sds((units, width))] + [sds((units, rows), F32)] * 2,
+        out_shape=[sds((units, width)), sds((units, rows), F32)],
         in_specs=[VMEM, VMEM, HBM],
-        out_specs=[VMEM] * 3,
+        out_specs=[VMEM] * 2,
+        input_output_aliases={1: 0},
         scratch_shapes=[pltpu.SemaphoreType.DMA((width // features,))],
-        compiler_params=pltpu.CompilerParams(vmem_limit_bytes=8 * 1024 * 1024),
+        compiler_params=pltpu.CompilerParams(vmem_limit_bytes=20 * 1024 * 1024),
         cost_estimate=pl.CostEstimate(
             flops=0, bytes_accessed=4 * up_weight.size, transcendentals=0
         ),
         name="load_up",
-    )(x, gate, pltpu.with_memory_space_constraint(up_weight, pltpu.HBM))
+    )(
+        x,
+        pltpu.with_memory_space_constraint(both, pltpu.VMEM),
+        pltpu.with_memory_space_constraint(up_weight, pltpu.HBM),
+    )
 
 
 def stack_kernel(places, *refs):
@@ -196,29 +209,24 @@
     )
 
 
-def grow(chunks, masks, gate_ref, up_ref, sums):
-    gate_vals, up_vals = sums
+def grow(chunks, masks, both_ref, sums):
     for ref, mask in zip(chunks, masks):
         own = columns(mask, ref.shape[1])
-        x = ref[...]
-        gate_part = lax.dot_general(gate_ref[:, own], x, NT, preferred_element_type=F32)
-        up_part = lax.dot_general(up_ref[:, own], x, NT, preferred_element_type=F32)
-        gate_vals = gate_vals + gate_part
-        up_vals = up_vals + up_part
-    return gate_vals, up_vals
+        sums = sums + lax.dot_general(both_ref[:, own], ref[...], NT, preferred_element_type=F32)
+    return sums
 
 
 def grow_kernel(masks, *refs):
-    chunks, (gate_ref, up_ref, gate_in, up_in, gate_out, up_out) = refs[:-6], refs[-6:]
-    sums = (gate_in[...], up_in[...])
-    gate_out[...], up_out[...] = grow(chunks, masks, gate_ref, up_ref, sums)
+    chunks, (both_ref, sums_in, sums_out) = refs[:-3], refs[-3:]
+    sums_out[...] = grow(chunks, masks, both_ref, sums_in[...])
 
 
 def expert_kernel(masks, out_masks, *refs):
     chunks = refs[: len(masks)]
-    gate_ref, up_ref, down_ref, gate_in, up_in, hidden_ref, out_ref = refs[len(masks) :]
-    sums = (gate_in[...], up_in[...])
-    gate_vals, up_vals = grow(chunks, masks, gate_ref, up_ref, sums)
+    both_ref, down_ref, sums_in, hidden_ref, out_ref = refs[len(masks) :]
+    sums = grow(chunks, masks, both_ref, sums_in[...])
+    units = sums.shape[0] // 2
+    gate_vals, up_vals = sums[:units], sums[units:]
     hidden = (gate_vals / (1.0 + jnp.exp(-gate_vals)) * up_vals).T.astype(BF16)
     hidden_ref[...] = hidden
     shrink(hidden, out_masks, down_ref, out_ref)
@@ -367,22 +375,22 @@
     ]
     near = [stack(mine, "stack_own", (), (1, 0))]
     far = [over_cores(near[0])]
-    up, *part = load_up(near[0], gate, up_weight)
+    both, part = load_up(near[0], gate, up_weight)
     down = pltpu.with_memory_space_constraint(down_weight[0], pltpu.VMEM)
-    near += [stack(pair, "stack_near", (up, down), (1, 0)) for pair in arriving]
+    near += [stack(pair, "stack_near", (both, down), (1, 0)) for pair in arriving]
     far += [over_cores(chunk) for chunk in near[1:]]
     part = local(
         functools.partial(grow_kernel, [1] + [j * CORES for j in range(1, chips)]),
         "grow",
-        [sds((units, rows), F32)] * 2,
-        (far[0], *near[1:], gate, up, *part),
+        sds((2 * units, rows), F32),
+        (far[0], *near[1:], both, part),
     )
     away = [j * CORES for j in range(1, chips)]
     hidden, given = local(
         functools.partial(expert_kernel, [m + 1 for m in away], [m + 1 for m in away]),
         "expert",
         [sds((rows, units)), sds((len(away) * rows, features))],
-        (*far[1:], gate, up, down, *part),
+        (*far[1:], both, down, part),
     )
 
     def shrunk(masks, name, after=()):

time: 32.3 us -> 32.3 us (level)
  no operation moved by 1% of the time
where the time goes in v2:
time: 32.3 us; the launch traced here: 32.1 us
  starting transfers between devices  16.6 us (51%)
  Pallas kernels  8.7 us (27%)
  waiting for transfers between devices  6.57 us (20%)
    ppermute x6, starting transfers between devices, over_ctx(): return lax.ppermute(array, 'ctx', swaps(ctx_size, mask))  10.2 us
    ppermute x4, starting transfers between devices, over_chips(): return lax.ppermute(array, 'tp', swaps(tp_size, mask * CORES))  5.87 us
    ppermute x4, waiting for transfers between devices, over_chips(): return lax.ppermute(array, 'tp', swaps(tp_size, mask * CORES))  2.97 us
    ppermute x6, waiting for transfers between devices, over_ctx(): return lax.ppermute(array, 'ctx', swaps(ctx_size, mask))  2.85 us
    pallas_call x15, Pallas kernels, local(): pl.pallas_call(kernel, out_shape=out_shape, in_specs=specs, out_specs=jax...  2.68 us
    pallas_call x1, Pallas kernels, load_up(): pl.pallas_call(load_up_kernel, out_shape=[sds((units, width)), sds((units...  2.05 us
    pallas_call x1, Pallas kernels, load_gate(): pl.pallas_call(functools.partial(load_gate_kernel, cuts), out_shape=[sds(...  1.88 us
    pallas_call x1, Pallas kernels, route(): pl.pallas_call(functools.partial(route_kernel, ctx_size, groups), out_sha...  1.2 us
  transfers between devices with their start and end apart: 14, of which 9 were waited for; matrix products, arithmetic and copies ran while one was open for 0% of the time, Pallas kernels for 18%

profile of v2, /device:TPU:0, one launch (start us, length us, event | category | flops | bytes accessed | tf_op | source)
XLA Modules:
  0.0 32.1 jit_solution(14421525921896258798)
XLA Ops:
  0.0 1.2 %route.1 = (f32[64,128]{1,0:T(8,128)S(1)}, bf16[16,1024]{1,0:T(8,128)(2,1)S(1)}, bf16[16,1024]{1,0:T(8,128)(2,1)S(1)}, bf16[16,1024]{1,0:T(8,128)(2,1)S(1)}, bf16[16,1024]{1,0:T(8,128)(2,1)S(1)}) custom-call(s32[8,128]{1,0:T(8,128)} %bitcast.8, f32[8,128]{1,0:T(8,128)} %bitcast.9, bf16[128,1024]{1,0:T(8,128)(2,1)} %tokens_hbm.1), custom_call_target="tpu_custom_call" | custom-call | tf_op jit(solution)/shard_map/route/pallas_call | solution.py:98
  1.2 4.1 %collective-permute-start = (bf16[16,1024]{1,0:T(8,128)(2,1)S(1)}, bf16[16,1024]{1,0:T(8,128)(2,1)S(1)}, u32[]{:S(2)}, u32[]{:S(2)}) collective-permute-start(bf16[16,1024]{1,0:T(8,128)(2,1)S(1)} %get-tuple-element.24), channel_id=1, source_target_pairs={{0,8},{4,12},{8,0},{12,4},{1,9},{5,13},{9,1},{13,5},{2,10},{6,14},... | collective-permute-start | bytes 98312 | tf_op jit(solution)/shard_map/ppermute | solution.py:341
  5.3 1.3 %collective-permute-start.1 = (bf16[16,1024]{1,0:T(8,128)(2,1)S(1)}, bf16[16,1024]{1,0:T(8,128)(2,1)S(1)}, u32[]{:S(2)}, u32[]{:S(2)}) collective-permute-start(bf16[16,1024]{1,0:T(8,128)(2,1)S(1)} %get-tuple-element.26), channel_id=1, source_target_pairs={{0,12},{4,8},{8,4},{12,0},{1,13},{5,9},{9,5},{13,1},{2,14},{6,10},... | collective-permute-start | bytes 98312 | tf_op jit(solution)/shard_map/ppermute | solution.py:341
  6.7 0.2 collective-permute-start.2
  6.9 1.9 %load_gate.1 = (bf16[768,4096]{1,0:T(8,128)(2,1)S(1)}, bf16[128,128]{1,0:T(8,128)(2,1)S(1)}) custom-call(bf16[1,384,4096]{2,1,0:T(8,128)(2,1)} %gate_hbm.1, f32[64,128]{1,0:T(8,128)S(1)} %get-tuple-element.21.combine_ref), custom_call_target="tpu_custom_call" | custom-call | bytes 6291456 | tf_op jit(solution)/shard_map/load_gate/pallas_call | solution.py:128
  8.8 0.0 collective-permute-done.refs_1_
  8.8 1.6 %collective-permute-start.3 = (bf16[32,1024]{1,0:T(8,128)(2,1)S(1)}, bf16[32,1024]{1,0:T(8,128)(2,1)S(1)}, u32[]{:S(2)}, u32[]{:S(2)}) collective-permute-start(bf16[32,1024]{1,0:T(8,128)(2,1)S(1)} %stack_half.2._.refs_0_), channel_id=1, source_target_pairs={{0,2},{1,3},{2,0},{3,1},{4,6},{5,7},{6,4},{7,5},{8,10},{9,11},{10,... | collective-permute-start | bytes 196616 | tf_op jit(solution)/shard_map/ppermute | solution.py:344
  10.4 0.7 %collective-permute-done.1.refs_2_ = bf16[16,1024]{1,0:T(8,128)(2,1)S(1)} collective-permute-done((bf16[16,1024]{1,0:T(8,128)(2,1)S(1)}, bf16[16,1024]{1,0:T(8,128)(2,1)S(1)}, u32[]{:S(2)}, u32[]{:S(2)}) %collective-permute-start.1) | collective-permute-done | bytes 32800 | tf_op jit(solution)/shard_map/ppermute | solution.py:341
  11.0 0.0 collective-permute-done.2.refs_3_
  11.0 1.6 %collective-permute-start.4 = (bf16[32,1024]{1,0:T(8,128)(2,1)S(1)}, bf16[32,1024]{1,0:T(8,128)(2,1)S(1)}, u32[]{:S(2)}, u32[]{:S(2)}) collective-permute-start(bf16[32,1024]{1,0:T(8,128)(2,1)S(1)} %stack_half.3.refs_1_), channel_id=1, source_target_pairs={{0,2},{1,3},{2,0},{3,1},{4,6},{5,7},{6,4},{7,5},{8,10},{9,11},{10,... | collective-permute-start | bytes 196616 | tf_op jit(solution)/shard_map/ppermute | solution.py:344
  12.6 0.0 copy-start
  12.6 0.1 collective-permute-start.6
  12.7 2.0 %load_up.1 = (bf16[768,4096]{1,0:T(8,128)(2,1)S(1)}, f32[768,64]{1,0:T(8,128)S(1)}) custom-call(bf16[64,1024]{1,0:T(8,128)(2,1)S(1)} %stack_own.1.x_ref, bf16[768,4096]{1,0:T(8,128)(2,1)S(1)} %get-tuple-element.25.refs_1_._, bf16[1,384,4096]{2,1,0:T(8,128)(2,1)} %up_hbm.1), custom_call_target="tpu_custom_call", output_to_operand_aliasing={{0}: (1, {})} | custom-call | bytes 6291456 | tf_op jit(solution)/shard_map/load_up/pallas_call | solution.py:175
  14.7 0.0 collective-permute-done.3.refs_2_
  14.8 0.6 %collective-permute-done.4.refs_3_ = bf16[32,1024]{1,0:T(8,128)(2,1)S(1)} collective-permute-done((bf16[32,1024]{1,0:T(8,128)(2,1)S(1)}, bf16[32,1024]{1,0:T(8,128)(2,1)S(1)}, u32[]{:S(2)}, u32[]{:S(2)}) %collective-permute-start.4) | collective-permute-done | bytes 65568 | tf_op jit(solution)/shard_map/ppermute | solution.py:344
  15.4 0.1 copy-done
  15.5 0.1 collective-permute-start.5
  15.5 0.0 collective-permute-done.6.refs_0_
  15.6 1.0 %grow.1.refs_3_ = f32[768,64]{1,0:T(8,128)S(1)} custom-call(bf16[64,1024]{1,0:T(8,128)(2,1)S(1)} %collective-permute-done.6.refs_0_, bf16[64,1024]{1,0:T(8,128)(2,1)S(1)} %stack_near.1.refs_1_, bf16[768,4096]{1,0:T(8,128)(2,1)S(1)} %get-tuple-element.28.refs_0_.refs_2_.refs_1_, f32[768,64]{1,0:T(8,128)S(1)} %get-tuple-element.29.refs_3_), custom_call_target="tpu_custom_call" | custom-call | bytes 6750208 | tf_op jit(solution)/shard_map/grow/pallas_call | solution.py:36
  16.5 0.4 %collective-permute-done.5.refs_0_ = bf16[64,1024]{1,0:T(8,128)(2,1)S(1)} collective-permute-done((bf16[64,1024]{1,0:T(8,128)(2,1)S(1)}, bf16[64,1024]{1,0:T(8,128)(2,1)S(1)}, u32[]{:S(2)}, u32[]{:S(2)}) %collective-permute-start.5) | collective-permute-done | bytes 131104 | tf_op jit(solution)/shard_map/ppermute | solution.py:347
  16.9 0.8 %expert.1 = (bf16[64,384]{1,0:T(8,128)(2,1)S(1)}, bf16[64,1024]{1,0:T(8,128)(2,1)S(1)}) custom-call(bf16[64,1024]{1,0:T(8,128)(2,1)S(1)} %collective-permute-done.5.refs_0_, bf16[768,4096]{1,0:T(8,128)(2,1)S(1)} %get-tuple-element.28.refs_0_.refs_2_.refs_1_, bf16[384,4096]{1,0:T(8,128)(2,1)S(1)} %bitcast.4, f32[768,64]{1,0:T(8,128)S(1)} %grow.1.refs_3_), custom_call_target="tpu_custom_call" | custom-call | bytes 9764864 | tf_op jit(solution)/shard_map/expert/pallas_call | solution.py:36
  17.7 0.2 collective-permute-start.7
  17.9 0.3 own_away.1.refs_0_.own_ref.own_away_ref
  18.2 0.3 given.1.refs_0_.refs_2_
  18.4 0.3 own.1.refs_0_.own_ref
  18.7 0.4 %collective-permute-done.7.refs_1_.other_ref.other_away_ref = bf16[64,1024]{1,0:T(8,128)(2,1)S(1)} collective-permute-done((bf16[64,1024]{1,0:T(8,128)(2,1)S(1)}, bf16[64,1024]{1,0:T(8,128)(2,1)S(1)}, u32[]{:S(2)}, u32[]{:S(2)}) %collective-permute-start.7) | collective-permute-done | bytes 131104 | tf_op jit(solution)/shard_map/ppermute | solution.py:347
  19.1 0.2 collective-permute-start.8
  19.4 1.5 %collective-permute-start.9 = (bf16[48,1024]{1,0:T(8,128)(2,1)S(1)}, bf16[48,1024]{1,0:T(8,128)(2,1)S(1)}, u32[]{:S(2)}, u32[]{:S(2)}) collective-permute-start(bf16[48,1024]{1,0:T(8,128)(2,1)S(1)} %pair.1), channel_id=1, source_target_pairs={{0,2},{1,3},{2,0},{3,1},{4,6},{5,7},{6,4},{7,5},{8,10},{9,11},{10,... | collective-permute-start | bytes 294920 | tf_op jit(solution)/shard_map/ppermute | solution.py:344
  20.8 0.0 collective-permute-done.8.other_ref
  20.9 1.8 %collective-permute-start.12 = (bf16[32,1024]{1,0:T(8,128)(2,1)S(1)}, bf16[32,1024]{1,0:T(8,128)(2,1)S(1)}, u32[]{:S(2)}, u32[]{:S(2)}) collective-permute-start(bf16[32,1024]{1,0:T(8,128)(2,1)S(1)} %tail.1), channel_id=1, source_target_pairs={{0,8},{4,12},{8,0},{12,4},{1,9},{5,13},{9,1},{13,5},{2,10},{6,14},... | collective-permute-start | bytes 196616 | tf_op jit(solution)/shard_map/ppermute | solution.py:341
  22.7 1.8 %collective-permute-done.9.refs_0_ = bf16[48,1024]{1,0:T(8,128)(2,1)S(1)} collective-permute-done((bf16[48,1024]{1,0:T(8,128)(2,1)S(1)}, bf16[48,1024]{1,0:T(8,128)(2,1)S(1)}, u32[]{:S(2)}, u32[]{:S(2)}) %collective-permute-start.9) | collective-permute-done | bytes 98336 | tf_op jit(solution)/shard_map/ppermute | solution.py:344
  24.5 2.2 %collective-permute-start.10 = (bf16[16,1024]{1,0:T(8,128)(2,1)S(1)}, bf16[16,1024]{1,0:T(8,128)(2,1)S(1)}, u32[]{:S(2)}, u32[]{:S(2)}) collective-permute-start(bf16[16,1024]{1,0:T(8,128)(2,1)S(1)} %get-tuple-element.32), channel_id=1, source_target_pairs={{0,12},{4,8},{8,4},{12,0},{1,13},{5,9},{9,5},{13,1},{2,14},{6,10},... | collective-permute-start | bytes 98312 | tf_op jit(solution)/shard_map/ppermute | solution.py:341
  26.8 0.4 %collective-permute-start.11 = (bf16[16,1024]{1,0:T(8,128)(2,1)S(1)}, bf16[16,1024]{1,0:T(8,128)(2,1)S(1)}, u32[]{:S(2)}, u32[]{:S(2)}) collective-permute-start(bf16[16,1024]{1,0:T(8,128)(2,1)S(1)} %get-tuple-element.33), channel_id=1, source_target_pairs={{0,4},{4,0},{8,12},{12,8},{1,5},{5,1},{9,13},{13,9},{2,6},{6,2},{1... | collective-permute-start | bytes 98312 | tf_op jit(solution)/shard_map/ppermute | solution.py:341
  27.2 0.1 collective-permute-done.12.in_ref
  27.3 1.3 %collective-permute-start.13 = (bf16[16,1024]{1,0:T(8,128)(2,1)S(1)}, bf16[16,1024]{1,0:T(8,128)(2,1)S(1)}, u32[]{:S(2)}, u32[]{:S(2)}) collective-permute-start(bf16[16,1024]{1,0:T(8,128)(2,1)S(1)} %get-tuple-element.36), channel_id=1, source_target_pairs={{0,2},{1,3},{2,0},{3,1},{4,6},{5,7},{6,4},{7,5},{8,10},{9,11},{10,... | collective-permute-start | bytes 98312 | tf_op jit(solution)/shard_map/ppermute | solution.py:344
  28.6 1.7 %collective-permute-done.10.refs_0_ = bf16[16,1024]{1,0:T(8,128)(2,1)S(1)} collective-permute-done((bf16[16,1024]{1,0:T(8,128)(2,1)S(1)}, bf16[16,1024]{1,0:T(8,128)(2,1)S(1)}, u32[]{:S(2)}, u32[]{:S(2)}) %collective-permute-start.10) | collective-permute-done | bytes 32800 | tf_op jit(solution)/shard_map/ppermute | solution.py:341
  30.3 0.4 %collective-permute-done.11.refs_1_ = bf16[16,1024]{1,0:T(8,128)(2,1)S(1)} collective-permute-done((bf16[16,1024]{1,0:T(8,128)(2,1)S(1)}, bf16[16,1024]{1,0:T(8,128)(2,1)S(1)}, u32[]{:S(2)}, u32[]{:S(2)}) %collective-permute-start.11) | collective-permute-done | bytes 32800 | tf_op jit(solution)/shard_map/ppermute | solution.py:341
  30.7 0.6 %collective-permute-done.13.refs_4_ = bf16[16,1024]{1,0:T(8,128)(2,1)S(1)} collective-permute-done((bf16[16,1024]{1,0:T(8,128)(2,1)S(1)}, bf16[16,1024]{1,0:T(8,128)(2,1)S(1)}, u32[]{:S(2)}, u32[]{:S(2)}) %collective-permute-start.13) | collective-permute-done | bytes 32800 | tf_op jit(solution)/shard_map/ppermute | solution.py:344
  31.2 0.9 %combine.1 = bf16[128,1024]{1,0:T(8,128)(2,1)} custom-call(bf16[128,128]{1,0:T(8,128)(2,1)S(1)} %get-tuple-element.22.mix_ref, bf16[16,1024]{1,0:T(8,128)(2,1)S(1)} %collective-permute-done.10.refs_0_, bf16[16,1024]{1,0:T(8,128)(2,1)S(1)} %collective-permute-done.11.refs_1_, bf16[16,1024]{1,0:T(8,128)(2,1)S(1)} %get-tuple-element.34.refs_2_, ...), custom_call_target="tpu_custom_call" | custom-call | tf_op jit(solution)/shard_map/combine/pallas_call | solution.py:319
  (10 shorter events, 0.1 us)
Async XLA Ops:
  1.2 7.6 %collective-permute-start = (bf16[16,1024]{1,0:T(8,128)(2,1)S(1)}, bf16[16,1024]{1,0:T(8,128)(2,1)S(1)}, u32[]{:S(2)}, u32[]{:S(2)}) collective-permute-start(bf16[16,1024]{1,0:T(8,128)(2,1)S(1)} %get-tuple-element.24), channel_id=1, source_target_pairs={{0,8},{4,12},{8,0},{12,4},{1,9},{5,13},{9,1},{13,5},{2,10},{6,14},... | collective-permute-start | bytes 98312 | tf_op jit(solution)/shard_map/ppermute | solution.py:341
  5.3 5.7 %collective-permute-start.1 = (bf16[16,1024]{1,0:T(8,128)(2,1)S(1)}, bf16[16,1024]{1,0:T(8,128)(2,1)S(1)}, u32[]{:S(2)}, u32[]{:S(2)}) collective-permute-start(bf16[16,1024]{1,0:T(8,128)(2,1)S(1)} %get-tuple-element.26), channel_id=1, source_target_pairs={{0,12},{4,8},{8,4},{12,0},{1,13},{5,9},{9,5},{13,1},{2,14},{6,10},... | collective-permute-start | bytes 98312 | tf_op jit(solution)/shard_map/ppermute | solution.py:341
  6.7 4.4 %collective-permute-start.2 = (bf16[16,1024]{1,0:T(8,128)(2,1)S(1)}, bf16[16,1024]{1,0:T(8,128)(2,1)S(1)}, u32[]{:S(2)}, u32[]{:S(2)}) collective-permute-start(bf16[16,1024]{1,0:T(8,128)(2,1)S(1)} %get-tuple-element.27), channel_id=1, source_target_pairs={{0,4},{4,0},{8,12},{12,8},{1,5},{5,1},{9,13},{13,9},{2,6},{6,2},{1... | collective-permute-start | bytes 98312 | tf_op jit(solution)/shard_map/ppermute | solution.py:341
  8.8 5.9 %collective-permute-start.3 = (bf16[32,1024]{1,0:T(8,128)(2,1)S(1)}, bf16[32,1024]{1,0:T(8,128)(2,1)S(1)}, u32[]{:S(2)}, u32[]{:S(2)}) collective-permute-start(bf16[32,1024]{1,0:T(8,128)(2,1)S(1)} %stack_half.2._.refs_0_), channel_id=1, source_target_pairs={{0,2},{1,3},{2,0},{3,1},{4,6},{5,7},{6,4},{7,5},{8,10},{9,11},{10,... | collective-permute-start | bytes 196616 | tf_op jit(solution)/shard_map/ppermute | solution.py:344
  11.0 4.3 %collective-permute-start.4 = (bf16[32,1024]{1,0:T(8,128)(2,1)S(1)}, bf16[32,1024]{1,0:T(8,128)(2,1)S(1)}, u32[]{:S(2)}, u32[]{:S(2)}) collective-permute-start(bf16[32,1024]{1,0:T(8,128)(2,1)S(1)} %stack_half.3.refs_1_), channel_id=1, source_target_pairs={{0,2},{1,3},{2,0},{3,1},{4,6},{5,7},{6,4},{7,5},{8,10},{9,11},{10,... | collective-permute-start | bytes 196616 | tf_op jit(solution)/shard_map/ppermute | solution.py:344
  12.6 2.9 %copy-start = (bf16[1,384,4096]{2,1,0:T(8,128)(2,1)S(1)}, bf16[1,384,4096]{2,1,0:T(8,128)(2,1)}, u32[]{:S(2)}) copy-start(bf16[1,384,4096]{2,1,0:T(8,128)(2,1)} %param.11) | copy-start | bytes 9437188
  12.6 2.9 %collective-permute-start.6 = (bf16[64,1024]{1,0:T(8,128)(2,1)S(1)}, bf16[64,1024]{1,0:T(8,128)(2,1)S(1)}, u32[]{:S(2)}, u32[]{:S(2)}) collective-permute-start(bf16[64,1024]{1,0:T(8,128)(2,1)S(1)} %stack_own.1.x_ref), channel_id=1, source_target_pairs={{0,1},{1,0},{2,3},{3,2},{4,5},{5,4},{6,7},{7,6},{8,9},{9,8},{10,11... | collective-permute-start | bytes 393224 | tf_op jit(solution)/shard_map/ppermute | solution.py:347
  15.5 1.4 %collective-permute-start.5 = (bf16[64,1024]{1,0:T(8,128)(2,1)S(1)}, bf16[64,1024]{1,0:T(8,128)(2,1)S(1)}, u32[]{:S(2)}, u32[]{:S(2)}) collective-permute-start(bf16[64,1024]{1,0:T(8,128)(2,1)S(1)} %stack_near.1.refs_1_), channel_id=1, source_target_pairs={{0,1},{1,0},{2,3},{3,2},{4,5},{5,4},{6,7},{7,6},{8,9},{9,8},{10,11... | collective-permute-start | bytes 393224 | tf_op jit(solution)/shard_map/ppermute | solution.py:347
  17.7 1.4 %collective-permute-start.7 = (bf16[64,1024]{1,0:T(8,128)(2,1)S(1)}, bf16[64,1024]{1,0:T(8,128)(2,1)S(1)}, u32[]{:S(2)}, u32[]{:S(2)}) collective-permute-start(bf16[64,1024]{1,0:T(8,128)(2,1)S(1)} %get-tuple-element.31), channel_id=1, source_target_pairs={{0,1},{1,0},{2,3},{3,2},{4,5},{5,4},{6,7},{7,6},{8,9},{9,8},{10,11... | collective-permute-start | bytes 393224 | tf_op jit(solution)/shard_map/ppermute | solution.py:347
  19.1 1.7 %collective-permute-start.8 = (bf16[64,1024]{1,0:T(8,128)(2,1)S(1)}, bf16[64,1024]{1,0:T(8,128)(2,1)S(1)}, u32[]{:S(2)}, u32[]{:S(2)}) collective-permute-start(bf16[64,1024]{1,0:T(8,128)(2,1)S(1)} %stack_given.1), channel_id=1, source_target_pairs={{0,1},{1,0},{2,3},{3,2},{4,5},{5,4},{6,7},{7,6},{8,9},{9,8},{10,11... | collective-permute-start | bytes 393224 | tf_op jit(solution)/shard_map/ppermute | solution.py:347
  19.4 5.1 %collective-permute-start.9 = (bf16[48,1024]{1,0:T(8,128)(2,1)S(1)}, bf16[48,1024]{1,0:T(8,128)(2,1)S(1)}, u32[]{:S(2)}, u32[]{:S(2)}) collective-permute-start(bf16[48,1024]{1,0:T(8,128)(2,1)S(1)} %pair.1), channel_id=1, source_target_pairs={{0,2},{1,3},{2,0},{3,1},{4,6},{5,7},{6,4},{7,5},{8,10},{9,11},{10,... | collective-permute-start | bytes 294920 | tf_op jit(solution)/shard_map/ppermute | solution.py:344
  20.9 6.5 %collective-permute-start.12 = (bf16[32,1024]{1,0:T(8,128)(2,1)S(1)}, bf16[32,1024]{1,0:T(8,128)(2,1)S(1)}, u32[]{:S(2)}, u32[]{:S(2)}) collective-permute-start(bf16[32,1024]{1,0:T(8,128)(2,1)S(1)} %tail.1), channel_id=1, source_target_pairs={{0,8},{4,12},{8,0},{12,4},{1,9},{5,13},{9,1},{13,5},{2,10},{6,14},... | collective-permute-start | bytes 196616 | tf_op jit(solution)/shard_map/ppermute | solution.py:341
  24.5 5.8 %collective-permute-start.10 = (bf16[16,1024]{1,0:T(8,128)(2,1)S(1)}, bf16[16,1024]{1,0:T(8,128)(2,1)S(1)}, u32[]{:S(2)}, u32[]{:S(2)}) collective-permute-start(bf16[16,1024]{1,0:T(8,128)(2,1)S(1)} %get-tuple-element.32), channel_id=1, source_target_pairs={{0,12},{4,8},{8,4},{12,0},{1,13},{5,9},{9,5},{13,1},{2,14},{6,10},... | collective-permute-start | bytes 98312 | tf_op jit(solution)/shard_map/ppermute | solution.py:341
  26.8 3.9 %collective-permute-start.11 = (bf16[16,1024]{1,0:T(8,128)(2,1)S(1)}, bf16[16,1024]{1,0:T(8,128)(2,1)S(1)}, u32[]{:S(2)}, u32[]{:S(2)}) collective-permute-start(bf16[16,1024]{1,0:T(8,128)(2,1)S(1)} %get-tuple-element.33), channel_id=1, source_target_pairs={{0,4},{4,0},{8,12},{12,8},{1,5},{5,1},{9,13},{13,9},{2,6},{6,2},{1... | collective-permute-start | bytes 98312 | tf_op jit(solution)/shard_map/ppermute | solution.py:341
  27.3 3.9 %collective-permute-start.13 = (bf16[16,1024]{1,0:T(8,128)(2,1)S(1)}, bf16[16,1024]{1,0:T(8,128)(2,1)S(1)}, u32[]{:S(2)}, u32[]{:S(2)}) collective-permute-start(bf16[16,1024]{1,0:T(8,128)(2,1)S(1)} %get-tuple-element.36), channel_id=1, source_target_pairs={{0,2},{1,3},{2,0},{3,1},{4,6},{5,7},{6,4},{7,5},{8,10},{9,11},{10,... | collective-permute-start | bytes 98312 | tf_op jit(solution)/shard_map/ppermute | solution.py:344

commit v3 on v2

--- a/solution.py
+++ b/solution.py
@@ -49,14 +49,18 @@
     return pl.ds(pl.multiple_of(at * features, features), features)
 
 
-def route_kernel(ctx_size, groups, ids_hbm, weight_hbm, tokens_hbm, combine_ref, *refs):
+def route_kernel(ctx_size, groups, cuts, ids_hbm, weight_hbm, tokens_hbm, combine_ref, *refs):
     *row_refs, ids_ref, weight_ref, tokens_ref, sems = refs
     copies = [
         pltpu.make_async_copy(source, target, sems.at[i])
-        for i, (source, target) in enumerate(
-            ((ids_hbm, ids_ref), (weight_hbm, weight_ref), (tokens_hbm, tokens_ref))
+        for i, (source, target) in enumerate(((ids_hbm, ids_ref), (weight_hbm, weight_ref)))
+    ]
+    step = tokens_ref.shape[0] // cuts
+    for c in range(cuts):
+        part = pl.ds(c * step, step)
+        copies.append(
+            pltpu.make_async_copy(tokens_hbm.at[part], tokens_ref.at[part], sems.at[2 + c])
         )
-    ]
     for copy in copies:
         copy.start()
     slots = groups * CAP
@@ -85,23 +89,24 @@
     running = jnp.dot(member.astype(BF16), before, preferred_element_type=F32)
     picked = jnp.where(running == slot, member, 0.0)
     combine_ref[...] = picked * weight
-    copies[2].wait()
+    for copy in copies[2:]:
+        copy.wait()
     rows = jnp.dot(picked.astype(BF16), tokens_ref[...], preferred_element_type=F32).astype(BF16)
     for s, ref in enumerate(row_refs):
         ref[...] = rows[s * slots : (s + 1) * slots]
 
 
-def route(ids_t, weight_t, tokens, ctx_size, groups):
+def route(ids_t, weight_t, tokens, ctx_size, groups, cuts=4):
     tok_rows, features = tokens.shape
     slots = groups * CAP
     args = (ids_t, weight_t, tokens)
     return pl.pallas_call(
-        functools.partial(route_kernel, ctx_size, groups),
+        functools.partial(route_kernel, ctx_size, groups, cuts),
         out_shape=[sds((ctx_size * slots, tok_rows), F32)] + [sds((slots, features))] * ctx_size,
         in_specs=[HBM] * 3,
         out_specs=[VMEM] * (ctx_size + 1),
         scratch_shapes=[pltpu.VMEM(a.shape, a.dtype) for a in args]
-        + [pltpu.SemaphoreType.DMA((3,))],
+        + [pltpu.SemaphoreType.DMA((2 + cuts,))],
         compiler_params=pltpu.CompilerParams(vmem_limit_bytes=4 * 1024 * 1024),
         name="route",
     )(*[pltpu.with_memory_space_constraint(a, pltpu.HBM) for a in args])
@@ -296,18 +301,15 @@
     count = len(order)
     back_refs, part_refs = refs[:count], refs[count:-3]
     back_refs = [back_refs[i] for i in order]
-    mix = mix_ref[...]
-    step = out_ref.shape[1] // cuts
+    late = group_sums(groups, [ref[...].astype(F32) for ref in part_refs])
+    back = jnp.concatenate([*[ref[...] for ref in back_refs], *late] * 2, axis=0)
+    step = out_ref.shape[0] // cuts
     copies = []
     for c in range(cuts):
         part = slice(c * step, (c + 1) * step)
-        parts = [ref[:, part].astype(F32) for ref in part_refs]
-        back = [ref[:, part] for ref in back_refs] + group_sums(groups, parts)
-        back = jnp.concatenate(back * 2, axis=0)
-        out_ref[:, part] = jnp.dot(mix, back, preferred_element_type=F32).astype(BF16)
-        copies.append(
-            pltpu.make_async_copy(out_ref.at[:, part], out_hbm.at[:, part], sems.at[c])
-        )
+        out = jnp.dot(mix_ref[part, :], back, preferred_element_type=F32)
+        out_ref[part, :] = out.astype(BF16)
+        copies.append(pltpu.make_async_copy(out_ref.at[part], out_hbm.at[part], sems.at[c]))
         copies[c].start()
     for copy in copies:
         copy.wait()

time: 32.3 us -> 32.3 us (level)
  no operation moved by 1% of the time
where the time goes in v3:
time: 32.3 us; the launch traced here: 32.1 us
  starting transfers between devices  16.6 us (51%)
  Pallas kernels  8.71 us (27%)
  waiting for transfers between devices  6.55 us (20%)
    ppermute x6, starting transfers between devices, over_ctx(): return lax.ppermute(array, 'ctx', swaps(ctx_size, mask))  10.2 us
    ppermute x4, starting transfers between devices, over_chips(): return lax.ppermute(array, 'tp', swaps(tp_size, mask * CORES))  5.86 us
    ppermute x4, waiting for transfers between devices, over_chips(): return lax.ppermute(array, 'tp', swaps(tp_size, mask * CORES))  2.95 us
    ppermute x6, waiting for transfers between devices, over_ctx(): return lax.ppermute(array, 'ctx', swaps(ctx_size, mask))  2.84 us
    pallas_call x15, Pallas kernels, local(): pl.pallas_call(kernel, out_shape=out_shape, in_specs=specs, out_specs=jax...  2.68 us
    pallas_call x1, Pallas kernels, load_up(): pl.pallas_call(load_up_kernel, out_shape=[sds((units, width)), sds((units...  2.05 us
    pallas_call x1, Pallas kernels, load_gate(): pl.pallas_call(functools.partial(load_gate_kernel, cuts), out_shape=[sds(...  1.88 us
    pallas_call x1, Pallas kernels, route(): pl.pallas_call(functools.partial(route_kernel, ctx_size, groups, cuts), o...  1.2 us
  transfers between devices with their start and end apart: 14, of which 9 were waited for; matrix products, arithmetic and copies ran while one was open for 0% of the time, Pallas kernels for 18%

profile of v3, /device:TPU:0, one launch (start us, length us, event | category | flops | bytes accessed | tf_op | source)
XLA Modules:
  0.0 32.1 jit_solution(13132218874164436940)
XLA Ops:
  0.0 1.2 %route.1 = (f32[64,128]{1,0:T(8,128)S(1)}, bf16[16,1024]{1,0:T(8,128)(2,1)S(1)}, bf16[16,1024]{1,0:T(8,128)(2,1)S(1)}, bf16[16,1024]{1,0:T(8,128)(2,1)S(1)}, bf16[16,1024]{1,0:T(8,128)(2,1)S(1)}) custom-call(s32[8,128]{1,0:T(8,128)} %bitcast.8, f32[8,128]{1,0:T(8,128)} %bitcast.9, bf16[128,1024]{1,0:T(8,128)(2,1)} %tokens_hbm.1), custom_call_target="tpu_custom_call" | custom-call | tf_op jit(solution)/shard_map/route/pallas_call | solution.py:103
  1.2 4.1 %collective-permute-start = (bf16[16,1024]{1,0:T(8,128)(2,1)S(1)}, bf16[16,1024]{1,0:T(8,128)(2,1)S(1)}, u32[]{:S(2)}, u32[]{:S(2)}) collective-permute-start(bf16[16,1024]{1,0:T(8,128)(2,1)S(1)} %get-tuple-element.24), channel_id=1, source_target_pairs={{0,8},{4,12},{8,0},{12,4},{1,9},{5,13},{9,1},{13,5},{2,10},{6,14},... | collective-permute-start | bytes 98312 | tf_op jit(solution)/shard_map/ppermute | solution.py:343
  5.3 1.3 %collective-permute-start.1 = (bf16[16,1024]{1,0:T(8,128)(2,1)S(1)}, bf16[16,1024]{1,0:T(8,128)(2,1)S(1)}, u32[]{:S(2)}, u32[]{:S(2)}) collective-permute-start(bf16[16,1024]{1,0:T(8,128)(2,1)S(1)} %get-tuple-element.26), channel_id=1, source_target_pairs={{0,12},{4,8},{8,4},{12,0},{1,13},{5,9},{9,5},{13,1},{2,14},{6,10},... | collective-permute-start | bytes 98312 | tf_op jit(solution)/shard_map/ppermute | solution.py:343
  6.7 0.2 collective-permute-start.2
  6.9 1.9 %load_gate.1 = (bf16[768,4096]{1,0:T(8,128)(2,1)S(1)}, bf16[128,128]{1,0:T(8,128)(2,1)S(1)}) custom-call(bf16[1,384,4096]{2,1,0:T(8,128)(2,1)} %gate_hbm.1, f32[64,128]{1,0:T(8,128)S(1)} %get-tuple-element.21.combine_ref), custom_call_target="tpu_custom_call" | custom-call | bytes 6291456 | tf_op jit(solution)/shard_map/load_gate/pallas_call | solution.py:133
  8.8 0.0 collective-permute-done.refs_1_
  8.8 1.6 %collective-permute-start.3 = (bf16[32,1024]{1,0:T(8,128)(2,1)S(1)}, bf16[32,1024]{1,0:T(8,128)(2,1)S(1)}, u32[]{:S(2)}, u32[]{:S(2)}) collective-permute-start(bf16[32,1024]{1,0:T(8,128)(2,1)S(1)} %stack_half.2._.refs_0_), channel_id=1, source_target_pairs={{0,2},{1,3},{2,0},{3,1},{4,6},{5,7},{6,4},{7,5},{8,10},{9,11},{10,... | collective-permute-start | bytes 196616 | tf_op jit(solution)/shard_map/ppermute | solution.py:346
  10.4 0.7 %collective-permute-done.1.refs_2_ = bf16[16,1024]{1,0:T(8,128)(2,1)S(1)} collective-permute-done((bf16[16,1024]{1,0:T(8,128)(2,1)S(1)}, bf16[16,1024]{1,0:T(8,128)(2,1)S(1)}, u32[]{:S(2)}, u32[]{:S(2)}) %collective-permute-start.1) | collective-permute-done | bytes 32800 | tf_op jit(solution)/shard_map/ppermute | solution.py:343
  11.0 0.0 collective-permute-done.2.refs_3_
  11.0 1.6 %collective-permute-start.4 = (bf16[32,1024]{1,0:T(8,128)(2,1)S(1)}, bf16[32,1024]{1,0:T(8,128)(2,1)S(1)}, u32[]{:S(2)}, u32[]{:S(2)}) collective-permute-start(bf16[32,1024]{1,0:T(8,128)(2,1)S(1)} %stack_half.3.refs_1_), channel_id=1, source_target_pairs={{0,2},{1,3},{2,0},{3,1},{4,6},{5,7},{6,4},{7,5},{8,10},{9,11},{10,... | collective-permute-start | bytes 196616 | tf_op jit(solution)/shard_map/ppermute | solution.py:346
  12.6 0.0 copy-start
  12.6 0.1 collective-permute-start.6
  12.7 2.0 %load_up.1 = (bf16[768,4096]{1,0:T(8,128)(2,1)S(1)}, f32[768,64]{1,0:T(8,128)S(1)}) custom-call(bf16[64,1024]{1,0:T(8,128)(2,1)S(1)} %stack_own.1.x_ref, bf16[768,4096]{1,0:T(8,128)(2,1)S(1)} %get-tuple-element.25.refs_1_._, bf16[1,384,4096]{2,1,0:T(8,128)(2,1)} %up_hbm.1), custom_call_target="tpu_custom_call", output_to_operand_aliasing={{0}: (1, {})} | custom-call | bytes 6291456 | tf_op jit(solution)/shard_map/load_up/pallas_call | solution.py:180
  14.8 0.0 collective-permute-done.3.refs_2_
  14.8 0.6 %collective-permute-done.4.refs_3_ = bf16[32,1024]{1,0:T(8,128)(2,1)S(1)} collective-permute-done((bf16[32,1024]{1,0:T(8,128)(2,1)S(1)}, bf16[32,1024]{1,0:T(8,128)(2,1)S(1)}, u32[]{:S(2)}, u32[]{:S(2)}) %collective-permute-start.4) | collective-permute-done | bytes 65568 | tf_op jit(solution)/shard_map/ppermute | solution.py:346
  15.4 0.1 copy-done
  15.5 0.1 collective-permute-start.5
  15.6 0.0 collective-permute-done.6.refs_0_
  15.6 1.0 %grow.1.refs_3_ = f32[768,64]{1,0:T(8,128)S(1)} custom-call(bf16[64,1024]{1,0:T(8,128)(2,1)S(1)} %collective-permute-done.6.refs_0_, bf16[64,1024]{1,0:T(8,128)(2,1)S(1)} %stack_near.1.refs_1_, bf16[768,4096]{1,0:T(8,128)(2,1)S(1)} %get-tuple-element.28.refs_0_.refs_2_.refs_1_, f32[768,64]{1,0:T(8,128)S(1)} %get-tuple-element.29.refs_3_), custom_call_target="tpu_custom_call" | custom-call | bytes 6750208 | tf_op jit(solution)/shard_map/grow/pallas_call | solution.py:36
  16.5 0.4 %collective-permute-done.5.refs_0_ = bf16[64,1024]{1,0:T(8,128)(2,1)S(1)} collective-permute-done((bf16[64,1024]{1,0:T(8,128)(2,1)S(1)}, bf16[64,1024]{1,0:T(8,128)(2,1)S(1)}, u32[]{:S(2)}, u32[]{:S(2)}) %collective-permute-start.5) | collective-permute-done | bytes 131104 | tf_op jit(solution)/shard_map/ppermute | solution.py:349
  16.9 0.8 %expert.1 = (bf16[64,384]{1,0:T(8,128)(2,1)S(1)}, bf16[64,1024]{1,0:T(8,128)(2,1)S(1)}) custom-call(bf16[64,1024]{1,0:T(8,128)(2,1)S(1)} %collective-permute-done.5.refs_0_, bf16[768,4096]{1,0:T(8,128)(2,1)S(1)} %get-tuple-element.28.refs_0_.refs_2_.refs_1_, bf16[384,4096]{1,0:T(8,128)(2,1)S(1)} %bitcast.4, f32[768,64]{1,0:T(8,128)S(1)} %grow.1.refs_3_), custom_call_target="tpu_custom_call" | custom-call | bytes 9764864 | tf_op jit(solution)/shard_map/expert/pallas_call | solution.py:36
  17.7 0.2 collective-permute-start.7
  17.9 0.3 own_away.1.refs_0_.own_ref.own_away_ref
  18.2 0.3 given.1.refs_0_.refs_2_
  18.4 0.3 own.1.refs_0_.own_ref
  18.7 0.4 %collective-permute-done.7.refs_1_.other_ref.other_away_ref = bf16[64,1024]{1,0:T(8,128)(2,1)S(1)} collective-permute-done((bf16[64,1024]{1,0:T(8,128)(2,1)S(1)}, bf16[64,1024]{1,0:T(8,128)(2,1)S(1)}, u32[]{:S(2)}, u32[]{:S(2)}) %collective-permute-start.7) | collective-permute-done | bytes 131104 | tf_op jit(solution)/shard_map/ppermute | solution.py:349
  19.1 0.2 collective-permute-start.8
  19.4 1.5 %collective-permute-start.9 = (bf16[48,1024]{1,0:T(8,128)(2,1)S(1)}, bf16[48,1024]{1,0:T(8,128)(2,1)S(1)}, u32[]{:S(2)}, u32[]{:S(2)}) collective-permute-start(bf16[48,1024]{1,0:T(8,128)(2,1)S(1)} %pair.1), channel_id=1, source_target_pairs={{0,2},{1,3},{2,0},{3,1},{4,6},{5,7},{6,4},{7,5},{8,10},{9,11},{10,... | collective-permute-start | bytes 294920 | tf_op jit(solution)/shard_map/ppermute | solution.py:346
  20.8 0.0 collective-permute-done.8.other_ref
  20.9 1.8 %collective-permute-start.12 = (bf16[32,1024]{1,0:T(8,128)(2,1)S(1)}, bf16[32,1024]{1,0:T(8,128)(2,1)S(1)}, u32[]{:S(2)}, u32[]{:S(2)}) collective-permute-start(bf16[32,1024]{1,0:T(8,128)(2,1)S(1)} %tail.1), channel_id=1, source_target_pairs={{0,8},{4,12},{8,0},{12,4},{1,9},{5,13},{9,1},{13,5},{2,10},{6,14},... | collective-permute-start | bytes 196616 | tf_op jit(solution)/shard_map/ppermute | solution.py:343
  22.7 1.8 %collective-permute-done.9.refs_0_ = bf16[48,1024]{1,0:T(8,128)(2,1)S(1)} collective-permute-done((bf16[48,1024]{1,0:T(8,128)(2,1)S(1)}, bf16[48,1024]{1,0:T(8,128)(2,1)S(1)}, u32[]{:S(2)}, u32[]{:S(2)}) %collective-permute-start.9) | collective-permute-done | bytes 98336 | tf_op jit(solution)/shard_map/ppermute | solution.py:346
  24.5 2.2 %collective-permute-start.10 = (bf16[16,1024]{1,0:T(8,128)(2,1)S(1)}, bf16[16,1024]{1,0:T(8,128)(2,1)S(1)}, u32[]{:S(2)}, u32[]{:S(2)}) collective-permute-start(bf16[16,1024]{1,0:T(8,128)(2,1)S(1)} %get-tuple-element.32), channel_id=1, source_target_pairs={{0,12},{4,8},{8,4},{12,0},{1,13},{5,9},{9,5},{13,1},{2,14},{6,10},... | collective-permute-start | bytes 98312 | tf_op jit(solution)/shard_map/ppermute | solution.py:343
  26.8 0.4 %collective-permute-start.11 = (bf16[16,1024]{1,0:T(8,128)(2,1)S(1)}, bf16[16,1024]{1,0:T(8,128)(2,1)S(1)}, u32[]{:S(2)}, u32[]{:S(2)}) collective-permute-start(bf16[16,1024]{1,0:T(8,128)(2,1)S(1)} %get-tuple-element.33), channel_id=1, source_target_pairs={{0,4},{4,0},{8,12},{12,8},{1,5},{5,1},{9,13},{13,9},{2,6},{6,2},{1... | collective-permute-start | bytes 98312 | tf_op jit(solution)/shard_map/ppermute | solution.py:343
  27.2 0.1 collective-permute-done.12.in_ref
  27.3 1.3 %collective-permute-start.13 = (bf16[16,1024]{1,0:T(8,128)(2,1)S(1)}, bf16[16,1024]{1,0:T(8,128)(2,1)S(1)}, u32[]{:S(2)}, u32[]{:S(2)}) collective-permute-start(bf16[16,1024]{1,0:T(8,128)(2,1)S(1)} %get-tuple-element.36), channel_id=1, source_target_pairs={{0,2},{1,3},{2,0},{3,1},{4,6},{5,7},{6,4},{7,5},{8,10},{9,11},{10,... | collective-permute-start | bytes 98312 | tf_op jit(solution)/shard_map/ppermute | solution.py:346
  28.6 1.7 %collective-permute-done.10.refs_0_ = bf16[16,1024]{1,0:T(8,128)(2,1)S(1)} collective-permute-done((bf16[16,1024]{1,0:T(8,128)(2,1)S(1)}, bf16[16,1024]{1,0:T(8,128)(2,1)S(1)}, u32[]{:S(2)}, u32[]{:S(2)}) %collective-permute-start.10) | collective-permute-done | bytes 32800 | tf_op jit(solution)/shard_map/ppermute | solution.py:343
  30.3 0.4 %collective-permute-done.11.refs_1_ = bf16[16,1024]{1,0:T(8,128)(2,1)S(1)} collective-permute-done((bf16[16,1024]{1,0:T(8,128)(2,1)S(1)}, bf16[16,1024]{1,0:T(8,128)(2,1)S(1)}, u32[]{:S(2)}, u32[]{:S(2)}) %collective-permute-start.11) | collective-permute-done | bytes 32800 | tf_op jit(solution)/shard_map/ppermute | solution.py:343
  30.7 0.5 %collective-permute-done.13.refs_4_ = bf16[16,1024]{1,0:T(8,128)(2,1)S(1)} collective-permute-done((bf16[16,1024]{1,0:T(8,128)(2,1)S(1)}, bf16[16,1024]{1,0:T(8,128)(2,1)S(1)}, u32[]{:S(2)}, u32[]{:S(2)}) %collective-permute-start.13) | collective-permute-done | bytes 32800 | tf_op jit(solution)/shard_map/ppermute | solution.py:346
  31.2 0.9 %combine.1 = bf16[128,1024]{1,0:T(8,128)(2,1)} custom-call(bf16[128,128]{1,0:T(8,128)(2,1)S(1)} %get-tuple-element.22.mix_ref, bf16[16,1024]{1,0:T(8,128)(2,1)S(1)} %collective-permute-done.10.refs_0_, bf16[16,1024]{1,0:T(8,128)(2,1)S(1)} %collective-permute-done.11.refs_1_, bf16[16,1024]{1,0:T(8,128)(2,1)S(1)} %get-tuple-element.34.refs_2_, ...), custom_call_target="tpu_custom_call" | custom-call | tf_op jit(solution)/shard_map/combine/pallas_call | solution.py:321
  (10 shorter events, 0.1 us)
Async XLA Ops:
  1.2 7.6 %collective-permute-start = (bf16[16,1024]{1,0:T(8,128)(2,1)S(1)}, bf16[16,1024]{1,0:T(8,128)(2,1)S(1)}, u32[]{:S(2)}, u32[]{:S(2)}) collective-permute-start(bf16[16,1024]{1,0:T(8,128)(2,1)S(1)} %get-tuple-element.24), channel_id=1, source_target_pairs={{0,8},{4,12},{8,0},{12,4},{1,9},{5,13},{9,1},{13,5},{2,10},{6,14},... | collective-permute-start | bytes 98312 | tf_op jit(solution)/shard_map/ppermute | solution.py:343
  5.3 5.7 %collective-permute-start.1 = (bf16[16,1024]{1,0:T(8,128)(2,1)S(1)}, bf16[16,1024]{1,0:T(8,128)(2,1)S(1)}, u32[]{:S(2)}, u32[]{:S(2)}) collective-permute-start(bf16[16,1024]{1,0:T(8,128)(2,1)S(1)} %get-tuple-element.26), channel_id=1, source_target_pairs={{0,12},{4,8},{8,4},{12,0},{1,13},{5,9},{9,5},{13,1},{2,14},{6,10},... | collective-permute-start | bytes 98312 | tf_op jit(solution)/shard_map/ppermute | solution.py:343
  6.7 4.4 %collective-permute-start.2 = (bf16[16,1024]{1,0:T(8,128)(2,1)S(1)}, bf16[16,1024]{1,0:T(8,128)(2,1)S(1)}, u32[]{:S(2)}, u32[]{:S(2)}) collective-permute-start(bf16[16,1024]{1,0:T(8,128)(2,1)S(1)} %get-tuple-element.27), channel_id=1, source_target_pairs={{0,4},{4,0},{8,12},{12,8},{1,5},{5,1},{9,13},{13,9},{2,6},{6,2},{1... | collective-permute-start | bytes 98312 | tf_op jit(solution)/shard_map/ppermute | solution.py:343
  8.8 5.9 %collective-permute-start.3 = (bf16[32,1024]{1,0:T(8,128)(2,1)S(1)}, bf16[32,1024]{1,0:T(8,128)(2,1)S(1)}, u32[]{:S(2)}, u32[]{:S(2)}) collective-permute-start(bf16[32,1024]{1,0:T(8,128)(2,1)S(1)} %stack_half.2._.refs_0_), channel_id=1, source_target_pairs={{0,2},{1,3},{2,0},{3,1},{4,6},{5,7},{6,4},{7,5},{8,10},{9,11},{10,... | collective-permute-start | bytes 196616 | tf_op jit(solution)/shard_map/ppermute | solution.py:346
  11.0 4.3 %collective-permute-start.4 = (bf16[32,1024]{1,0:T(8,128)(2,1)S(1)}, bf16[32,1024]{1,0:T(8,128)(2,1)S(1)}, u32[]{:S(2)}, u32[]{:S(2)}) collective-permute-start(bf16[32,1024]{1,0:T(8,128)(2,1)S(1)} %stack_half.3.refs_1_), channel_id=1, source_target_pairs={{0,2},{1,3},{2,0},{3,1},{4,6},{5,7},{6,4},{7,5},{8,10},{9,11},{10,... | collective-permute-start | bytes 196616 | tf_op jit(solution)/shard_map/ppermute | solution.py:346
  12.6 2.9 %copy-start = (bf16[1,384,4096]{2,1,0:T(8,128)(2,1)S(1)}, bf16[1,384,4096]{2,1,0:T(8,128)(2,1)}, u32[]{:S(2)}) copy-start(bf16[1,384,4096]{2,1,0:T(8,128)(2,1)} %param.11) | copy-start | bytes 9437188
  12.6 2.9 %collective-permute-start.6 = (bf16[64,1024]{1,0:T(8,128)(2,1)S(1)}, bf16[64,1024]{1,0:T(8,128)(2,1)S(1)}, u32[]{:S(2)}, u32[]{:S(2)}) collective-permute-start(bf16[64,1024]{1,0:T(8,128)(2,1)S(1)} %stack_own.1.x_ref), channel_id=1, source_target_pairs={{0,1},{1,0},{2,3},{3,2},{4,5},{5,4},{6,7},{7,6},{8,9},{9,8},{10,11... | collective-permute-start | bytes 393224 | tf_op jit(solution)/shard_map/ppermute | solution.py:349
  15.5 1.4 %collective-permute-start.5 = (bf16[64,1024]{1,0:T(8,128)(2,1)S(1)}, bf16[64,1024]{1,0:T(8,128)(2,1)S(1)}, u32[]{:S(2)}, u32[]{:S(2)}) collective-permute-start(bf16[64,1024]{1,0:T(8,128)(2,1)S(1)} %stack_near.1.refs_1_), channel_id=1, source_target_pairs={{0,1},{1,0},{2,3},{3,2},{4,5},{5,4},{6,7},{7,6},{8,9},{9,8},{10,11... | collective-permute-start | bytes 393224 | tf_op jit(solution)/shard_map/ppermute | solution.py:349
  17.7 1.4 %collective-permute-start.7 = (bf16[64,1024]{1,0:T(8,128)(2,1)S(1)}, bf16[64,1024]{1,0:T(8,128)(2,1)S(1)}, u32[]{:S(2)}, u32[]{:S(2)}) collective-permute-start(bf16[64,1024]{1,0:T(8,128)(2,1)S(1)} %get-tuple-element.31), channel_id=1, source_target_pairs={{0,1},{1,0},{2,3},{3,2},{4,5},{5,4},{6,7},{7,6},{8,9},{9,8},{10,11... | collective-permute-start | bytes 393224 | tf_op jit(solution)/shard_map/ppermute | solution.py:349
  19.1 1.7 %collective-permute-start.8 = (bf16[64,1024]{1,0:T(8,128)(2,1)S(1)}, bf16[64,1024]{1,0:T(8,128)(2,1)S(1)}, u32[]{:S(2)}, u32[]{:S(2)}) collective-permute-start(bf16[64,1024]{1,0:T(8,128)(2,1)S(1)} %stack_given.1), channel_id=1, source_target_pairs={{0,1},{1,0},{2,3},{3,2},{4,5},{5,4},{6,7},{7,6},{8,9},{9,8},{10,11... | collective-permute-start | bytes 393224 | tf_op jit(solution)/shard_map/ppermute | solution.py:349
  19.4 5.1 %collective-permute-start.9 = (bf16[48,1024]{1,0:T(8,128)(2,1)S(1)}, bf16[48,1024]{1,0:T(8,128)(2,1)S(1)}, u32[]{:S(2)}, u32[]{:S(2)}) collective-permute-start(bf16[48,1024]{1,0:T(8,128)(2,1)S(1)} %pair.1), channel_id=1, source_target_pairs={{0,2},{1,3},{2,0},{3,1},{4,6},{5,7},{6,4},{7,5},{8,10},{9,11},{10,... | collective-permute-start | bytes 294920 | tf_op jit(solution)/shard_map/ppermute | solution.py:346
  20.9 6.4 %collective-permute-start.12 = (bf16[32,1024]{1,0:T(8,128)(2,1)S(1)}, bf16[32,1024]{1,0:T(8,128)(2,1)S(1)}, u32[]{:S(2)}, u32[]{:S(2)}) collective-permute-start(bf16[32,1024]{1,0:T(8,128)(2,1)S(1)} %tail.1), channel_id=1, source_target_pairs={{0,8},{4,12},{8,0},{12,4},{1,9},{5,13},{9,1},{13,5},{2,10},{6,14},... | collective-permute-start | bytes 196616 | tf_op jit(solution)/shard_map/ppermute | solution.py:343
  24.5 5.8 %collective-permute-start.10 = (bf16[16,1024]{1,0:T(8,128)(2,1)S(1)}, bf16[16,1024]{1,0:T(8,128)(2,1)S(1)}, u32[]{:S(2)}, u32[]{:S(2)}) collective-permute-start(bf16[16,1024]{1,0:T(8,128)(2,1)S(1)} %get-tuple-element.32), channel_id=1, source_target_pairs={{0,12},{4,8},{8,4},{12,0},{1,13},{5,9},{9,5},{13,1},{2,14},{6,10},... | collective-permute-start | bytes 98312 | tf_op jit(solution)/shard_map/ppermute | solution.py:343
  26.8 3.9 %collective-permute-start.11 = (bf16[16,1024]{1,0:T(8,128)(2,1)S(1)}, bf16[16,1024]{1,0:T(8,128)(2,1)S(1)}, u32[]{:S(2)}, u32[]{:S(2)}) collective-permute-start(bf16[16,1024]{1,0:T(8,128)(2,1)S(1)} %get-tuple-element.33), channel_id=1, source_target_pairs={{0,4},{4,0},{8,12},{12,8},{1,5},{5,1},{9,13},{13,9},{2,6},{6,2},{1... | collective-permute-start | bytes 98312 | tf_op jit(solution)/shard_map/ppermute | solution.py:343
  27.3 3.9 %collective-permute-start.13 = (bf16[16,1024]{1,0:T(8,128)(2,1)S(1)}, bf16[16,1024]{1,0:T(8,128)(2,1)S(1)}, u32[]{:S(2)}, u32[]{:S(2)}) collective-permute-start(bf16[16,1024]{1,0:T(8,128)(2,1)S(1)} %get-tuple-element.36), channel_id=1, source_target_pairs={{0,2},{1,3},{2,0},{3,1},{4,6},{5,7},{6,4},{7,5},{8,10},{9,11},{10,... | collective-permute-start | bytes 98312 | tf_op jit(solution)/shard_map/ppermute | solution.py:346
